TPU v7x, 512 devices: a whole 4x8x8 slice. The times are simulated.
512 devices in a mesh: recv: 32 (over z, y_lo), tm: 16 (over x, y_hi, core).
Axes of the slice: x: 4, y: 8 (y_hi: 2, y_lo: 4; y = y_hi * 4 + y_lo), z: 8, core: 2. Of those that a mesh axis runs over, the one named last changes fastest.
Arguments:
- spectra: bfloat16 [2, 512, 256, 512], P(None, 'tm', 'recv'), may hold values from -6 to 6
- owners: int32 [4], replicated, may hold values from 0 to 31
- source_slots: int32 [4, 8], replicated, may hold values from 0 to 7, as said below
Outputs:
- correlations: float32 [32, 256, 512], P('tm', 'recv')
Inputs may be any that keep to these rules, and one draw needn't show every extreme that they name: Block k of sources lies among the channels of recv index owners[k]. `source_slots`: the 8 slots of one block are distinct.
All inputs are finite; a program needn't handle non-finite values.
Results may differ from a plain program's by a relative error of at most 0.0019.
Values may be sent and summed in bfloat16 or wider, within the bound.
No kernel may reach another device: no remote copies, remote signals or barrier semaphores. Data moves between devices by JAX's collectives and lax.ppermute only.
A program may use at most 64 MiB of HBM per device.

v0:
```python
import math

import jax
import jax.numpy as jnp
from jax import lax
from jax.sharding import PartitionSpec as P

HALF = 64
STEPS = 4


epsilon = 1e-05


def broadcast(value, axis, source):
    kept = jnp.where(lax.axis_index(axis) == source, value, 0).astype(value.dtype)
    return lax.psum(kept, axis)


def band_matrix(length, half_width):
    positions = lax.iota(jnp.int32, length)
    near = (jnp.abs(positions[:, None] - positions[None, :]) <= half_width).astype(jnp.float32)
    return near / jnp.sum(near, axis=0, keepdims=True)


def transform_tables(length):
    positions = lax.iota(jnp.int32, length)
    phase = positions[:, None] * positions[None, :] % length
    angle = phase.astype(jnp.float32) * (2.0 * math.pi / length)
    return (jnp.cos(angle), jnp.sin(angle))


def inverse_lags(cross_real, cross_imag, cosine, sine):
    length = cross_real.shape[-1]
    high = lax.Precision.HIGHEST
    flat_real = cross_real.reshape(-1, length)
    flat_imag = cross_imag.reshape(-1, length)
    lag_terms = jnp.dot(
        flat_real, cosine, precision=high, preferred_element_type=jnp.float32
    ) - jnp.dot(flat_imag, sine, precision=high, preferred_element_type=jnp.float32)
    return (lag_terms / length).reshape(cross_real.shape)


def per_device(spectra, owners, source_slots):
    length = spectra.shape[3]
    width = spectra.shape[2]
    band_table = band_matrix(length, HALF)
    parts = spectra.astype(jnp.float32)
    energy = parts[0] * parts[0] + parts[1] * parts[1]
    smooth = jnp.dot(
        energy.reshape(-1, length),
        band_table,
        precision=lax.Precision.HIGHEST,
        preferred_element_type=jnp.float32,
    ).reshape(energy.shape)
    whitened = (parts * lax.rsqrt(smooth + epsilon)[None]).astype(jnp.bfloat16)
    positions = lax.iota(jnp.int32, width)
    real_parts = []
    imag_parts = []
    for step in range(STEPS):
        selector = (source_slots[step][:, None] == positions[None, :]).astype(jnp.bfloat16)
        picked = jnp.einsum(
            "sr,cwrf->cwsf", selector, whitened, preferred_element_type=jnp.float32
        ).astype(jnp.bfloat16)
        arrived = broadcast(picked, "recv", owners[step])
        real_parts.append(
            jnp.einsum("wsf,wrf->srf", arrived[0], whitened[0], preferred_element_type=jnp.float32)
            + jnp.einsum(
                "wsf,wrf->srf", arrived[1], whitened[1], preferred_element_type=jnp.float32
            )
        )
        imag_parts.append(
            jnp.einsum("wsf,wrf->srf", arrived[0], whitened[1], preferred_element_type=jnp.float32)
            - jnp.einsum(
                "wsf,wrf->srf", arrived[1], whitened[0], preferred_element_type=jnp.float32
            )
        )
    cross_real = jnp.concatenate(real_parts, axis=0)
    cross_imag = jnp.concatenate(imag_parts, axis=0)
    cosine, sine = transform_tables(length)
    return lax.psum_scatter(
        inverse_lags(cross_real, cross_imag, cosine, sine), "tm", scatter_dimension=0, tiled=True
    )


def solution(mesh):
    in_specs = (P(None, "tm", "recv", None), P(), P())
    out_specs = P("tm", "recv", None)
    return jax.shard_map(
        per_device, mesh=mesh, in_specs=in_specs, out_specs=out_specs, check_vma=False
    )
```

profile of v0, /device:TPU:1, one launch (start us, length us, event | category | flops | bytes accessed | tf_op | source)
XLA Modules:
  0.0 529.7 jit_solution(2936204565653662733)
XLA Ops:
  6.7 1.4 fusion.64
  8.1 1.2 convert_element_type.41
  9.3 1.1 fusion
  13.0 1.2 fusion.10
  14.2 1.2 fusion.4
  15.4 1.2 fusion.6
  16.6 1.2 fusion.8
  17.7 0.2 reduce-scatter.2.cloned.1.call-start
  18.0 0.8 copy.85
  18.9 0.8 copy.83
  19.7 305.9 %all-reduce.3.cloned.1.call-done = (bf16[2,32,8,512]{3,2,1,0:T(8,128)(2,1)}, bf16[2,32,8,512]{3,2,1,0:T(8,128)(2,1)}, bf16[2,32,8,512]{3,2,1,0:T(8,128)(2,1)}, bf16[2,32,8,512]{3,2,1,0:T(8,128)(2,1)}) async-done(((bf16[2,32,8,512]{3,2,1,0:T(8,128)(2,1)}, bf16[2,32,8,512]{3,2,1,0:T(8,128)(2,1)}, bf16[2,32,8,512]{3,2,1,0:T(8,128)(2,1)}, bf16[2,32,8,512]{3,2,1,0:T(8,128)(2,1)}), ...) | async-done | bytes 2097168 | tf_op jit(solution)/shard_map/psum | solution.py:17
  325.6 2.1 slice_bitcast_fusion.4
  327.7 1.8 copy.84
  329.5 1.8 copy.88
  331.3 2.0 fusion.69
  333.3 2.1 fusion.70
  335.4 2.0 fusion.65
  337.5 2.1 fusion.66
  339.6 0.9 slice_bitcast_fusion
  340.5 1.8 copy.92
  342.4 2.1 fusion.67
  344.4 2.0 fusion.71
  346.4 1.8 copy.96
  348.3 2.0 fusion.68
  350.3 2.0 fusion.72
  352.3 1.8 copy.86
  354.1 3.6 subtract_bitcast_fusion.3
  357.7 2.2 copy.119
  359.9 3.0 copy.90
  362.9 3.9 subtract_bitcast_fusion.2
  366.8 2.8 copy.120
  369.7 3.6 add_bitcast_fusion.3
  373.3 2.9 copy.99
  376.2 3.6 add_bitcast_fusion.2
  379.8 2.8 copy.100
  382.6 1.8 copy.94
  384.4 3.7 add_bitcast_fusion.1
  388.1 2.8 copy.101
  390.9 1.8 copy.98
  392.7 4.0 add_bitcast_fusion
  396.7 2.2 copy.102
  398.8 3.6 subtract_bitcast_fusion.1
  402.4 2.3 copy.121
  404.7 3.6 subtract_bitcast_fusion
  408.4 2.2 copy.122
  410.6 5.2 fusion.17
  415.8 5.7 %fusion.2 = f32[32,8,512]{2,1,0:T(8,128)} fusion(f32[256,512]{1,0:T(8,128)S(1)} %fusion.17, f32[8,8,512]{2,1,0:T(8,128)S(1)} %copy.122, f32[8,8,512]{2,1,0:T(8,128)S(1)} %copy.121, f32[8,8,512]{2,1,0:T(8,128)S(1)} %copy-done.6, f32[8,8,512]{2,1,0:T(8,128)S(1)} %copy.119), kind=kOutput, calls=%fused_computation.21 | convolution fusion | flops 809631744 | bytes 1572864 | tf_op jit(solution)/shard_map/dot_general | solution.py:40
  421.5 101.4 %reduce-scatter.2.cloned.1.call-done = f32[2,8,512]{2,1,0:T(8,128)} async-done(((f32[32,8,512]{2,1,0:T(8,128)}), f32[2,8,512]{2,1,0:T(8,128)}) %reduce-scatter.2.cloned.1.call-update) | async-done | bytes 32784 | tf_op jit(solution)/shard_map/reduce_scatter | solution.py:81
  (29 shorter events, 0.4 us)
Async XLA Ops:
  6.5 319.1 %all-reduce.3.cloned.1.call-start = ((), (), s32[]{:S(2)}) async-start(), calls=%async_computation.2 | async-start | bytes 4194304 | tf_op jit(solution)/shard_map/psum | solution.py:17
  9.3 1.2 copy-start.3
  9.3 1.3 copy-start.10
  17.7 505.2 %reduce-scatter.2.cloned.1.call-start = ((), (), s32[]{:S(2)}) async-start(), calls=%async_computation.1 | async-start | bytes 557056 | tf_op jit(solution)/shard_map/reduce_scatter | solution.py:81
  331.3 2.0 copy-start.2
  337.5 2.1 copy-start.4
  337.5 2.1 copy-start.5
  373.3 2.9 copy-start.1
  402.4 2.3 copy-start
  408.4 2.2 copy-start.7
  408.4 2.3 copy-start.8
  408.4 2.3 copy-start.9
  410.6 5.2 copy-start.6
Sparse Core Ops, SparseCore 0:
  17.9 307.6 all-reduce.2
  421.7 101.1 reduce-scatter.1
where the time goes:
time: 531 us; the launch traced here: 530 us
  waiting for transfers between devices  407 us (77%)
  matrix products  62.7 us (12%)
  local copies, waits for them, and re-layouts  42.1 us (8%)
  between operations  16.1 us (3%)
    psum x1, waiting for transfers between devices, broadcast(): return lax.psum(kept, axis)  306 us
    reduce_scatter x1, waiting for transfers between devices, per_device(): lax.psum_scatter(inverse_lags(cross_real, cross_imag, cosine, sine), 'tm'...  101 us
    dot_general x4, matrix products, per_device(): jnp.einsum('wsf,wrf->srf', arrived[1], whitened[1], preferred_element_typ...  14.8 us
    dot_general x4, matrix products, per_device(): jnp.einsum('wsf,wrf->srf', arrived[1], whitened[0], preferred_element_typ...  14.7 us
    squeeze x6, local copies, waits for them, and re-layouts, per_device(): arrived[1]  11.4 us
    add x4, local copies, waits for them, and re-layouts, per_device(): jnp.einsum('wsf,wrf->srf', arrived[0], whitened[0], preferred_element_typ...  10.7 us
  transfers between devices with their start and end apart: 2, of which 2 were waited for; matrix products, arithmetic and copies ran while one was open for 0% of the time, Pallas kernels for 0%

commit v1 on v0

v1 whole, which is shorter than its diff:
```python
import functools

import jax
import jax.numpy as jnp
import ml_dtypes
import numpy as np
from jax import lax
from jax.experimental import pallas as pl
from jax.experimental.pallas import tpu as pltpu
from jax.sharding import PartitionSpec as P

F = 512
HALF = 64
N_RECV = 32
N_TM = 16
RECV_DEV = 8
WIN = 32
PAIRS = 8
EPSILON = 1e-05
INTERPRET = False

f32 = jnp.float32
bf16 = jnp.bfloat16


def bin_order():
    order = []
    for j in range(N_RECV):
        mine = [PAIRS * j + p for p in range(PAIRS)]
        order += mine + [F // 2 if f == 0 else F - f for f in mine]
    return np.array(order)


def tables():
    index = np.arange(F)
    near = np.abs(index[:, None] - index[None, :]) <= HALF
    counts = near.sum(0).astype(np.float32)[None, :]
    order = (bin_order()[:, None] == index[None, :]).astype(ml_dtypes.bfloat16)
    c, w, r = np.meshgrid(np.arange(2), np.arange(WIN), np.arange(RECV_DEV), indexing="ij")
    goes_to = (r * 2 * WIN + c * WIN + w).reshape(-1)
    lanes = (goes_to[:, None] == np.arange(2 * WIN * RECV_DEV)[None, :]).astype(ml_dtypes.bfloat16)
    lag = np.arange(F)
    wave = np.zeros((N_RECV, PAIRS, 2, F))
    for j in range(N_RECV):
        for p in range(PAIRS):
            f = PAIRS * j + p
            angle = 2 * np.pi * ((f * lag) % F) / F
            if f == 0:
                wave[j, p, 0] = 1.0
                wave[j, p, 1] = 1.0 - 2.0 * (lag % 2)
            else:
                wave[j, p, 0] = np.cos(angle)
                wave[j, p, 1] = -np.sin(angle)
    wave = (wave / F).reshape(F, F)
    high = wave.astype(ml_dtypes.bfloat16)
    low = (wave - high.astype(np.float64)).astype(ml_dtypes.bfloat16)
    blocks = [m.astype(ml_dtypes.bfloat16).reshape(F // 8, 8, F) for m in (near, order, lanes, high, low)]
    return [jnp.asarray(m) for m in (*blocks, counts)]


def table(ref):
    return ref[...].reshape(F, F)


def dot(a, b):
    return lax.dot_general(a, b, (((1,), (0,)), ((), ())), preferred_element_type=f32)


def dot_nt(a, b):
    return lax.dot_general(a, b, (((1,), (1,)), ((), ())), preferred_element_type=f32)


def whiten_kernel(x_ref, near_ref, order_ref, lanes_ref, counts_ref, y_ref):
    rows = WIN * RECV_DEV
    re = x_ref[0].astype(f32).reshape(rows, F)
    im = x_ref[1].astype(f32).reshape(rows, F)
    energy = re * re + im * im
    near = table(near_ref)
    first = energy.astype(bf16)
    rest = energy - first.astype(f32)
    second = rest.astype(bf16)
    third = (rest - second.astype(f32)).astype(bf16)
    total = dot(first, near) + (dot(second, near) + dot(third, near))
    scale = lax.rsqrt(total / counts_ref[...] + EPSILON)
    white = jnp.concatenate([(re * scale).astype(bf16), (im * scale).astype(bf16)], axis=0)
    turned = dot_nt(table(order_ref), white).astype(bf16)
    y_ref[...] = dot(turned, table(lanes_ref)).astype(bf16).reshape(y_ref.shape)


def cross_kernel(owners_ref, slots_ref, place_ref, y_ref, z_ref, wide):
    for g in range(4):
        wide[g] = y_ref[:, :, 128 * g : 128 * (g + 1)].astype(f32).reshape(wide.shape[1:])
    lane8 = lax.broadcasted_iota(jnp.int32, (8, 128), 1)
    odd_source = (lax.broadcasted_iota(jnp.int32, (8, 128), 0) // 2) % 2 == 1
    even_rows, odd_rows = [], []
    for t in range(N_TM):
        keys = []
        for s in (2 * t, 2 * t + 1):
            slot = slots_ref[s // 8, s % 8]
            keys.append((slot // 2) * N_RECV + owners_ref[s // 8] + 128 * (slot % 2))
        key = jnp.where(odd_source, keys[1], keys[0])
        even_rows.append(key == lane8)
        odd_rows.append(key - 128 == lane8)
    pick = jnp.concatenate(
        [
            jnp.concatenate([m.astype(f32) for m in even_rows], axis=0),
            jnp.concatenate([m.astype(f32) for m in odd_rows], axis=0),
        ],
        axis=1,
    ).astype(bf16)

    row = lax.broadcasted_iota(jnp.int32, (128, 128), 0)
    lane = lax.broadcasted_iota(jnp.int32, (128, 128), 1)
    second_part = (row // 4) % 2 == 1
    same_half = (row % 2) == (lane // 64)
    real_lane = (lane // 32) % 2 == 0
    low_lane = lane < 64
    is_first = place_ref[0] == 0
    halves = []
    for p in range(PAIRS):
        sides = []
        picked = []
        for sign in range(2):
            blocks = [
                wide.at[g][pl.ds(p + PAIRS * sign, N_RECV, stride=2 * PAIRS), :]
                for g in range(4)
            ]
            side = jnp.concatenate(blocks, axis=0)
            stacked = jnp.concatenate(
                [jnp.where(low_lane, side, 0.0), jnp.where(low_lane, 0.0, side)], axis=0
            ).astype(bf16)
            sides.append(side.astype(bf16))
            found = dot(pick, stacked)
            source = found + pltpu.roll(found, 64, 1)
            turned = pltpu.roll(source, 32, 1)
            turned = jnp.where(real_lane, -turned, turned)
            if sign:
                turned = -turned
            if p == 0:
                if sign:
                    first_part = jnp.where(is_first, 0.0, source)
                    turned = jnp.where(is_first, source, turned)
                else:
                    first_part = source
                    turned = jnp.where(is_first, 0.0, turned)
            else:
                first_part = source
            left = jnp.where(second_part, turned, first_part)
            picked.append(jnp.where(same_half, left, 0.0).astype(bf16))
        out = dot_nt(jnp.concatenate(picked, axis=1), jnp.concatenate(sides, axis=1))
        halves.append(out.reshape(N_TM, 8, 128))
        if p % 2:
            z_ref[:, 8 * (p - 1) : 8 * (p + 1), :] = jnp.concatenate(halves, axis=1).astype(bf16)
            halves = []


def gather_kernel(z_ref, q_ref, total):
    total[...] = jnp.sum(z_ref[...].astype(f32), axis=0)
    parts = [total[pl.ds(k, 16, stride=4), :] for k in range(4)]
    tall = jnp.concatenate(parts + [jnp.zeros((64, 128), f32)], axis=0)
    turned = tall.T
    for r in range(RECV_DEV):
        g = r // 2
        q_ref[:, r, :] = turned[N_RECV * g : N_RECV * (g + 1), :]


def lags_kernel(q_ref, high_ref, low_ref, out_ref):
    lane = lax.broadcasted_iota(jnp.int32, (8, 128), 1) // 16
    odd_row = lax.broadcasted_iota(jnp.int32, (8, 128), 0) % 2 == 1
    rows = []
    for s in range(2):
        tiles = []
        for q in range(4):
            tile = jnp.zeros((8, 128), f32)
            for i in range(8):
                block = q_ref[8 * q + i]
                here = []
                for k in (2 * s, 2 * s + 1):
                    shift = (16 * (i - k)) % 128
                    here.append(pltpu.roll(block, shift, 1) if shift else block)
                tile = jnp.where(lane == i, jnp.where(odd_row, here[1], here[0]), tile)
            tiles.append(tile)
        rows.append(jnp.concatenate(tiles, axis=1))
    value = jnp.concatenate(rows, axis=0)
    first = value.astype(bf16)
    second = (value - first.astype(f32)).astype(bf16)
    both = dot(jnp.concatenate([first, second], axis=0), table(high_ref))
    out_ref[...] = (both[:16] + (both[16:] + dot(first, table(low_ref)))).reshape(out_ref.shape)


def call(kernel, shape, dtype, operands, scratch=(), scalars=0):
    vmem = pl.BlockSpec(memory_space=pltpu.VMEM)
    smem = pl.BlockSpec(memory_space=pltpu.SMEM)
    return pl.pallas_call(
        kernel,
        out_shape=jax.ShapeDtypeStruct(shape, dtype),
        in_specs=[smem] * scalars + [vmem] * (len(operands) - scalars),
        out_specs=vmem,
        scratch_shapes=list(scratch),
        compiler_params=pltpu.CompilerParams(vmem_limit_bytes=32 << 20),
        interpret=INTERPRET,
    )(*operands)


def whiten(spectra):
    near, order, lanes, _, _, counts = tables()
    return call(
        whiten_kernel,
        (N_RECV, 2 * PAIRS, 2 * WIN * RECV_DEV),
        bf16,
        [spectra, near, order, lanes, counts],
    )


def cross(owners, source_slots, place, channels):
    return call(
        cross_kernel,
        (N_TM, 8 * PAIRS, 128),
        bf16,
        [owners, source_slots, place, channels],
        [pltpu.VMEM((4, N_RECV * 2 * PAIRS, 128), f32)],
        scalars=3,
    )


def gather(partial):
    return call(gather_kernel, (N_RECV, 8, 128), f32, [partial], [pltpu.VMEM((64, 128), f32)])


def lags(dofs):
    _, _, _, high, low, _ = tables()
    return call(lags_kernel, (2, RECV_DEV, F), f32, [dofs, high, low])


def per_device(spectra, owners, source_slots):
    exchange = functools.partial(lax.all_to_all, split_axis=0, concat_axis=0, tiled=True)
    place = lax.axis_index("recv").astype(jnp.int32).reshape(1)
    channels = exchange(whiten(spectra), "recv")
    partial = exchange(cross(owners, source_slots, place, channels), "tm")
    return lags(exchange(gather(partial), "recv"))


def solution(mesh):
    in_specs = (P(None, "tm", "recv", None), P(), P())
    out_specs = P("tm", "recv", None)
    return jax.shard_map(
        per_device, mesh=mesh, in_specs=in_specs, out_specs=out_specs, check_vma=False
    )
```

time: 531 us -> 78.8 us (0.15)
  waiting for transfers between devices: 407 us -> 14.9 us
  matrix products: 62.7 us -> 0 us
  blocking collectives: 0 us -> 37.7 us
  local copies, waits for them, and re-layouts: 42.1 us -> 4.87 us
  between operations: 16.1 us -> 0.06 us
  starting transfers between devices: 0.22 us -> 14.3 us
  Pallas kernels: 0 us -> 6.59 us
    psum x1 -> x0, waiting for transfers between devices: 306 us -> none  [broadcast(): return lax.psum(kept, axis)]
    reduce_scatter x1 -> x0, waiting for transfers between devices: 101 us -> none  [per_device(): lax.psum_scatter(inverse_lags(cross_real, cross_imag, cosine, sine), 'tm'...]
    dot_general x23 -> x0, matrix products: 62.7 us -> none  [the longest x4 14.8 us: per_device(): jnp.einsum('wsf,wrf->srf', arrived[1], whitened[1], preferred_element_typ...]
    all_to_all x0 -> x2, blocking collectives: none -> 37.7 us  [the longest x1 21.2 us: per_device(): partial = exchange(cross(owners, source_slots, place, channels), 'tm')]
    squeeze x13 -> x0, local copies, waits for them, and re-layouts: 20.4 us -> none  [the longest x6 11.4 us: per_device(): arrived[1]]
    all_to_all x0 -> x1, waiting for transfers between devices: none -> 14.9 us  [per_device(): channels = exchange(whiten(spectra), 'recv')]
    all_to_all x0 -> x1, starting transfers between devices: none -> 14.3 us  [per_device(): channels = exchange(whiten(spectra), 'recv')]
    add x4 -> x0, local copies, waits for them, and re-layouts: 10.7 us -> none  [per_device(): jnp.einsum('wsf,wrf->srf', arrived[0], whitened[0], preferred_element_typ...]
  transfers between devices with their start and end apart: 2 -> 1, of which waited for: 2 -> 1; matrix products, arithmetic and copies ran while one was open for 0% -> 0% of each run, Pallas kernels for 0% -> 0%
where the time goes in v1:
time: 78.8 us; the launch traced here: 78.4 us
  blocking collectives  37.7 us (48%)
  waiting for transfers between devices  14.9 us (19%)
  starting transfers between devices  14.3 us (18%)
  Pallas kernels  6.59 us (8%)
  local copies, waits for them, and re-layouts  4.87 us (6%)
    all_to_all x1, blocking collectives, per_device(): partial = exchange(cross(owners, source_slots, place, channels), 'tm')  21.2 us
    all_to_all x1, blocking collectives, per_device(): return lags(exchange(gather(partial), 'recv'))  16.5 us
    all_to_all x1, waiting for transfers between devices, per_device(): channels = exchange(whiten(spectra), 'recv')  14.9 us
    all_to_all x1, starting transfers between devices, per_device(): channels = exchange(whiten(spectra), 'recv')  14.3 us
    pallas_call x4, Pallas kernels, call(): pl.pallas_call(kernel, out_shape=jax.ShapeDtypeStruct(shape, dtype), in_s...  6.59 us
    unnamed x18, local copies, waits for them, and re-layouts  4.87 us
  transfers between devices with their start and end apart: 1, of which 1 were waited for; matrix products, arithmetic and copies ran while one was open for 0% of the time, Pallas kernels for 0%

profile of v1, /device:TPU:1, one launch (start us, length us, event | category | flops | bytes accessed | tf_op | source)
XLA Modules:
  0.0 78.4 jit_solution(6046989145608475723)
XLA Ops:
  0.0 0.0 copy-start.7
  0.0 0.7 copy-done.7
  0.7 0.0 copy-start.2
  0.7 1.0 %copy-done.2 = bf16[2,32,8,512]{3,2,1,0:T(8,128)(2,1)S(1)} copy-done((bf16[2,32,8,512]{3,2,1,0:T(8,128)(2,1)S(1)}, bf16[2,32,8,512]{3,2,1,0:T(8,128)(2,1)}, u32[]{:S(2)}) %copy-start.2) | copy-done | bytes 524312
  1.7 0.0 copy-start.3
  1.7 1.0 %copy-done.3 = bf16[64,8,512]{2,1,0:T(8,128)(2,1)S(1)} copy-done((bf16[64,8,512]{2,1,0:T(8,128)(2,1)S(1)}, bf16[64,8,512]{2,1,0:T(8,128)(2,1)}, u32[]{:S(2)}) %copy-start.3) | copy-done | bytes 524312
  2.8 0.0 copy-start.4
  2.8 1.0 %copy-done.4 = bf16[64,8,512]{2,1,0:T(8,128)(2,1)S(1)} copy-done((bf16[64,8,512]{2,1,0:T(8,128)(2,1)S(1)}, bf16[64,8,512]{2,1,0:T(8,128)(2,1)}, u32[]{:S(2)}) %copy-start.4) | copy-done | bytes 524312
  3.8 0.0 copy-start.5
  3.8 1.0 %copy-done.5 = bf16[64,8,512]{2,1,0:T(8,128)(2,1)S(1)} copy-done((bf16[64,8,512]{2,1,0:T(8,128)(2,1)S(1)}, bf16[64,8,512]{2,1,0:T(8,128)(2,1)}, u32[]{:S(2)}) %copy-start.5) | copy-done | bytes 524312
  4.9 2.1 %shard_map.91 = bf16[32,16,512]{2,1,0:T(8,128)(2,1)} custom-call(bf16[2,32,8,512]{3,2,1,0:T(8,128)(2,1)S(1)} %copy-done.2, bf16[64,8,512]{2,1,0:T(8,128)(2,1)S(1)} %copy-done.3, bf16[64,8,512]{2,1,0:T(8,128)(2,1)S(1)} %copy-done.4, bf16[64,8,512]{2,1,0:T(8,128)(2,1)S(1)} %copy-done.5, f32[1,512]{1,0:T(1,128)S(1)} %copy-done.7), custom_call_target="tpu_custom_call" | custom-call | tf_op jit(solution)/shard_map/pallas_call | solution.py:194
  7.0 14.3 %all-to-all-start = ((bf16[32,16,512]{2,1,0:T(8,128)(2,1)}), bf16[32,16,512]{2,1,0:T(8,128)(2,1)S(1)}, u32[]{:S(2)}, u32[]{:S(2)}) async-start(bf16[32,16,512]{2,1,0:T(8,128)(2,1)} %shard_map.91), calls=%async_computation | async-start | bytes 1048576 | tf_op jit(solution)/shard_map/all_to_all | solution.py:238
  21.3 0.0 copy-start.6
  21.3 0.0 copy-start.8
  21.3 14.9 %all-to-all-done.y_ref = bf16[32,16,512]{2,1,0:T(8,128)(2,1)S(1)} async-done(((bf16[32,16,512]{2,1,0:T(8,128)(2,1)}), bf16[32,16,512]{2,1,0:T(8,128)(2,1)S(1)}, u32[]{:S(2)}, u32[]{:S(2)}) %all-to-all-start) | async-done | bytes 524320 | tf_op jit(solution)/shard_map/all_to_all | solution.py:238
  36.2 0.0 copy-done.6
  36.2 0.0 copy-done.8
  36.2 3.3 %shard_map.92 = bf16[16,64,128]{2,1,0:T(8,128)(2,1)S(1)} custom-call(s32[4]{0:T(128)S(1)} %copy-done.8, s32[4,8]{1,0:T(4,128)S(1)} %copy-done.6, s32[1]{0:T(128)} %bitcast.place_ref, bf16[32,16,512]{2,1,0:T(8,128)(2,1)S(1)} %all-to-all-done.y_ref), custom_call_target="tpu_custom_call" | custom-call | tf_op jit(solution)/shard_map/pallas_call | solution.py:194
  39.5 0.0 copy-start
  39.5 0.0 copy-start.1
  39.5 21.2 %all_to_all.15.z_ref = bf16[16,64,128]{2,1,0:T(8,128)(2,1)S(1)} all-to-all(bf16[16,64,128]{2,1,0:T(8,128)(2,1)S(1)} %shard_map.92), channel_id=1, replica_groups=mesh['recv'=32,'tm'=16] {'tm'}, dimensions={0} | all-to-all | bytes 524288 | tf_op jit(solution)/shard_map/all_to_all | solution.py:239
  60.7 0.2 shard_map.93
  60.8 16.5 %all_to_all.16.q_ref = f32[32,8,128]{2,1,0:T(8,128)S(1)} all-to-all(f32[32,8,128]{2,1,0:T(8,128)S(1)} %shard_map.93), channel_id=1, replica_groups=mesh['recv'=32,'tm'=16] {'recv'}, dimensions={0} | all-to-all | bytes 262144 | tf_op jit(solution)/shard_map/all_to_all | solution.py:240
  77.4 0.0 copy-done
  77.4 0.0 copy-done.1
  77.4 1.0 %shard_map.94 = f32[2,8,512]{2,1,0:T(8,128)} custom-call(f32[32,8,128]{2,1,0:T(8,128)S(1)} %all_to_all.16.q_ref, bf16[64,8,512]{2,1,0:T(8,128)(2,1)S(1)} %copy-done, bf16[64,8,512]{2,1,0:T(8,128)(2,1)S(1)} %copy-done.1), custom_call_target="tpu_custom_call" | custom-call | tf_op jit(solution)/shard_map/pallas_call | solution.py:194
Async XLA Ops:
  0.0 0.7 copy-start.7
  0.7 1.0 %copy-start.2 = (bf16[2,32,8,512]{3,2,1,0:T(8,128)(2,1)S(1)}, bf16[2,32,8,512]{3,2,1,0:T(8,128)(2,1)}, u32[]{:S(2)}) copy-start(bf16[2,32,8,512]{3,2,1,0:T(8,128)(2,1)} %x_ref.1) | copy-start | bytes 1572868
  1.7 1.0 %copy-start.3 = (bf16[64,8,512]{2,1,0:T(8,128)(2,1)S(1)}, bf16[64,8,512]{2,1,0:T(8,128)(2,1)}, u32[]{:S(2)}) copy-start(bf16[64,8,512]{2,1,0:T(8,128)(2,1)} %constant.18.clone.near_ref) | copy-start | bytes 1572868
  2.8 1.0 %copy-start.4 = (bf16[64,8,512]{2,1,0:T(8,128)(2,1)S(1)}, bf16[64,8,512]{2,1,0:T(8,128)(2,1)}, u32[]{:S(2)}) copy-start(bf16[64,8,512]{2,1,0:T(8,128)(2,1)} %constant.19.clone.order_ref) | copy-start | bytes 1572868
  3.8 1.0 %copy-start.5 = (bf16[64,8,512]{2,1,0:T(8,128)(2,1)S(1)}, bf16[64,8,512]{2,1,0:T(8,128)(2,1)}, u32[]{:S(2)}) copy-start(bf16[64,8,512]{2,1,0:T(8,128)(2,1)} %constant.20.clone.lanes_ref) | copy-start | bytes 1572868
  7.0 29.2 %all-to-all-start = ((bf16[32,16,512]{2,1,0:T(8,128)(2,1)}), bf16[32,16,512]{2,1,0:T(8,128)(2,1)S(1)}, u32[]{:S(2)}, u32[]{:S(2)}) async-start(bf16[32,16,512]{2,1,0:T(8,128)(2,1)} %shard_map.91), calls=%async_computation | async-start | bytes 1048576 | tf_op jit(solution)/shard_map/all_to_all | solution.py:238
  21.3 14.9 %copy-start.6 = (s32[4,8]{1,0:T(4,128)S(1)}, s32[4,8]{1,0:T(4,128)}, u32[]{:S(2)}) copy-start(s32[4,8]{1,0:T(4,128)} %slots_ref.1) | copy-start | bytes 388
  21.3 14.9 %copy-start.8 = (s32[4]{0:T(128)S(1)}, s32[4]{0:T(128)}, u32[]{:S(2)}) copy-start(s32[4]{0:T(128)} %owners_ref.1) | copy-start | bytes 52
  39.5 37.9 %copy-start = (bf16[64,8,512]{2,1,0:T(8,128)(2,1)S(1)}, bf16[64,8,512]{2,1,0:T(8,128)(2,1)}, u32[]{:S(2)}) copy-start(bf16[64,8,512]{2,1,0:T(8,128)(2,1)} %constant.22.clone.high_ref) | copy-start | bytes 1572868
  39.5 37.9 %copy-start.1 = (bf16[64,8,512]{2,1,0:T(8,128)(2,1)S(1)}, bf16[64,8,512]{2,1,0:T(8,128)(2,1)}, u32[]{:S(2)}) copy-start(bf16[64,8,512]{2,1,0:T(8,128)(2,1)} %constant.23.clone.low_ref) | copy-start | bytes 1572868

commit v2 on v0

v2 whole, which is shorter than its diff:
```python
import functools

import jax
import jax.numpy as jnp
import ml_dtypes
import numpy as np
from jax import lax
from jax.experimental import pallas as pl
from jax.experimental.pallas import tpu as pltpu
from jax.sharding import Mesh
from jax.sharding import PartitionSpec as P

F = 512
HALF = 64
N_RECV = 32
N_TM = 16
RECV_DEV = 8
WIN = 32
PAIRS = 8
EPSILON = 1e-05
INTERPRET = False

RECV = ("z", "y_lo")
TM = ("x", "y_hi", "core")
SIZES = {"z": 8, "y_lo": 4, "x": 4, "y_hi": 2, "core": 2}

f32 = jnp.float32
bf16 = jnp.bfloat16


def transform_table():
    lag = np.arange(F)
    wave = np.zeros((2, PAIRS, N_RECV, F))
    for j in range(N_RECV):
        for p in range(PAIRS):
            f = PAIRS * j + p
            angle = 2 * np.pi * ((f * lag) % F) / F
            if f == 0:
                wave[0, p, j] = 1.0
                wave[1, p, j] = 1.0 - 2.0 * (lag % 2)
            else:
                wave[0, p, j] = np.cos(angle)
                wave[1, p, j] = -np.sin(angle)
    wave = (wave / F).reshape(F // 8, 8, F)
    high = wave.astype(ml_dtypes.bfloat16)
    low = (wave - high.astype(np.float64)).astype(ml_dtypes.bfloat16)
    return jnp.asarray(high), jnp.asarray(low)


def dot(a, b):
    return lax.dot_general(a, b, (((1,), (0,)), ((), ())), preferred_element_type=f32)


def dot_nt(a, b):
    return lax.dot_general(a, b, (((1,), (1,)), ((), ())), preferred_element_type=f32)


def iota(shape, dim):
    return lax.broadcasted_iota(jnp.int32, shape, dim)


def ones_where(mask):
    return jnp.where(mask, 1.0, 0.0).astype(bf16)


def tm_place(t):
    return (t // 4) * 4 + (t % 2) * 2 + (t // 2) % 2


def band():
    gap = iota((128, 128), 0) - iota((128, 128), 1)
    inside = ones_where(jnp.abs(gap) <= HALF)
    above = ones_where(gap >= HALF)
    below = ones_where(gap <= -HALF)
    nothing = jnp.zeros((128, 128), bf16)
    pieces = {0: inside, 1: above, -1: below}
    rows = [
        jnp.concatenate([pieces.get(b - a, nothing) for b in range(4)], axis=1) for a in range(4)
    ]
    return jnp.concatenate(rows, axis=0)


def source_picker(owners_ref, slots_ref, pick_ref):
    sub = iota((8, 128), 0)
    lane = iota((8, 128), 1)
    for odd in range(2):
        for half in range(2):
            key = jnp.zeros((8, 128), jnp.int32)
            for t in range(N_TM):
                place = tm_place(t)
                if place // 8 != half:
                    continue
                s = 2 * t + odd
                channel = owners_ref[s // 8] * RECV_DEV + slots_ref[s // 8, s % 8]
                key = jnp.where(sub == place % 8, channel, key)
            found = jnp.concatenate(
                [jnp.where(key == lane, 1.0, 0.0), jnp.where(key == lane + 128, 1.0, 0.0)], axis=1
            )
            for dof in range(2):
                row = (2 * odd + dof) * N_TM + 8 * half
                pick_ref[row : row + 8, :] = found


def whiten_kernel(
    x_hbm, owners_hbm, slots_hbm, y_ref, pick_ref, x_ref, owners_ref, slots_ref, tall, pick, sems
):
    is_first = lax.axis_index(RECV) == 0
    copies = [
        pltpu.make_async_copy(owners_hbm, owners_ref, sems.at[4]),
        pltpu.make_async_copy(slots_hbm, slots_ref, sems.at[5]),
    ]
    for c in range(2):
        for part in range(2):
            here = pl.ds(part * WIN // 2, WIN // 2)
            copies.append(
                pltpu.make_async_copy(x_hbm.at[c, here], x_ref.at[c, here], sems.at[2 * c + part])
            )
    for copy in copies:
        copy.start()

    near = band()
    bins = iota((8, F), 1)
    counts = (jnp.minimum(bins + HALF, F - 1) - jnp.maximum(bins - HALF, 0) + 1).astype(f32)
    row = iota((256, 256), 0)
    column = iota((256, 256), 1)
    forward = ones_where(row == column)
    backward = ones_where((row + column) % 256 == 0)
    source_row = iota((F, 128), 0)
    goes_to = (source_row % 8) * 64 + source_row // 8
    lane = iota((F, 128), 1)
    lanes = jnp.concatenate([ones_where(goes_to == lane + 128 * b) for b in range(4)], axis=1)

    for copy in copies:
        copy.wait()
    source_picker(owners_ref, slots_ref, pick)
    pick[64:80, :] = jnp.full((16, 256), jnp.where(is_first, 1.0, 0.0), f32)
    pick_ref[...] = pick[...].astype(bf16)

    rows = WIN * RECV_DEV
    re = x_ref[0].astype(f32).reshape(rows, F)
    im = x_ref[1].astype(f32).reshape(rows, F)
    energy = re * re + im * im
    first = energy.astype(bf16)
    rest = energy - first.astype(f32)
    second = rest.astype(bf16)
    third = (rest - second.astype(f32)).astype(bf16)
    total = dot(first, near) + (dot(second, near) + dot(third, near))
    scale = lax.rsqrt(total * (1.0 / counts)[:1] + EPSILON)
    white = jnp.concatenate([(re * scale).astype(bf16), (im * scale).astype(bf16)], axis=0)
    ahead = dot(dot_nt(forward, white[:, :256]).astype(bf16), lanes)
    behind = dot(dot_nt(backward, white[:, 256:]).astype(bf16), lanes)
    low = iota((256, 128), 1) < 64
    for g in range(4):
        one = ahead[:, 128 * g : 128 * (g + 1)]
        two = behind[:, 128 * g : 128 * (g + 1)]
        tall[pl.ds(2 * g, 256, stride=8), :] = jnp.where(low, one, pltpu.roll(two, 64, 1))
        tall[pl.ds(2 * g + 1, 256, stride=8), :] = jnp.where(low, pltpu.roll(one, 64, 1), two)
    y_ref[...] = tall[...].astype(bf16).reshape(y_ref.shape)


def cross_kernel(pick_ref, y_ref, z_ref, wide):
    pick = pick_ref[:64, :]
    is_first = pick_ref[64:80, :128].astype(f32)[:1] > 0.5
    row = iota((64, 128), 0)
    lane = iota((64, 128), 1)
    imaginary = (row // N_TM) % 2 == 1
    real_lane = (lane // 32) % 2 == 0
    ahead = lane < 64
    sign = jnp.where(real_lane == ahead, -1.0, 1.0)
    for p in range(PAIRS):
        if p % 2 == 0:
            two = y_ref[:, 8 * p : 8 * p + 16, :].astype(f32)
        side = two[:, 8 * (p % 2) : 8 * (p % 2) + 8, :].reshape(256, 128).astype(bf16)
        source = dot(pick, side)
        turned = sign * jnp.where(real_lane, pltpu.roll(source, 96, 1), pltpu.roll(source, 32, 1))
        left = jnp.where(imaginary, turned, source)
        if p == 0:
            ends = jnp.where(imaginary == ahead, 0.0, source)
            left = jnp.where(is_first, ends, left)
        out = dot_nt(left.astype(bf16), side)
        for q in range(4):
            for h in range(2):
                wide.at[h][pl.ds(8 * q + p, N_TM, stride=32), :] = out[
                    N_TM * q : N_TM * (q + 1), 128 * h : 128 * (h + 1)
                ]
    for h in range(2):
        z_ref[:, :, 128 * h : 128 * (h + 1)] = wide[h].astype(bf16).reshape(8, 64, 128)


def gather_kernel(z_ref, q_ref, tall, flat):
    total = jnp.sum(z_ref[...].astype(f32), axis=0)
    for h in range(2):
        block = total[:, 128 * h : 128 * (h + 1)]
        tall[128 * h : 128 * (h + 1), :] = jnp.concatenate([block, jnp.zeros_like(block)], axis=0).T
    group = iota((N_RECV, 128), 1) // 32
    for h in range(2):
        channels = [tall[pl.ds(4 * h + r, N_RECV, stride=8), :] for r in range(4)]
        for y in range(2):
            packed = jnp.zeros((N_RECV, 128), f32)
            for r in range(4):
                moved = channels[r]
                if r != y:
                    moved = pltpu.roll(moved, (32 * (r - y)) % 128, 1)
                packed = jnp.where(group == r, moved, packed)
            flat.at[h][pl.ds(y, N_RECV, stride=2), :] = packed
    for h in range(2):
        q_ref[:, h, :] = flat[h]


def lags_kernel(q_ref, high_ref, low_ref, out_ref, flat, turned, mixed):
    for h in range(2):
        flat.at[h][...] = q_ref[:, h, :]
    sums = []
    for h in range(2):
        sums.append(
            flat.at[h][pl.ds(0, N_RECV, stride=2), :] + flat.at[h][pl.ds(1, N_RECV, stride=2), :]
        )
    turned[...] = jnp.concatenate(sums + [jnp.zeros((64, 128), f32)], axis=0).T
    group = iota((8, 128), 1) // 32
    rows = [[], []]
    for q in range(4):
        tiles = [jnp.zeros((8, 128), f32) for _ in range(2)]
        for i in range(4):
            block = turned[pl.ds(4 * q + i, 8, stride=16), :]
            for h in range(2):
                moved = pltpu.roll(block, (32 * (i - h)) % 128, 1) if i != h else block
                tiles[h] = jnp.where(group == i, moved, tiles[h])
        for h in range(2):
            rows[h].append(tiles[h])
    value = jnp.concatenate([jnp.concatenate(r, axis=1) for r in rows], axis=0)
    first = value.astype(bf16)
    second = (value - first.astype(f32)).astype(bf16)
    high = high_ref[...].reshape(F, F)
    low = low_ref[...].reshape(F, F)
    both = dot(jnp.concatenate([first, second], axis=0), high)
    lags = both[:16] + (both[16:] + dot(first, low))
    for b in range(4):
        mixed.at[b][...] = lags[:, 128 * b : 128 * (b + 1)]
    for s in range(2):
        for b in range(4):
            out_ref[s, :, 128 * b : 128 * (b + 1)] = mixed.at[b][pl.ds(s, 8, stride=2), :]


VMEM = pl.BlockSpec(memory_space=pltpu.VMEM)
SMEM = pl.BlockSpec(memory_space=pltpu.SMEM)
HBM = pl.BlockSpec(memory_space=pl.ANY)


def call(kernel, outs, operands, specs, scratch=(), grant=32):
    return pl.pallas_call(
        kernel,
        out_shape=outs,
        in_specs=specs,
        out_specs=jax.tree.map(lambda _: VMEM, outs),
        scratch_shapes=list(scratch),
        compiler_params=pltpu.CompilerParams(vmem_limit_bytes=grant << 20),
        interpret=INTERPRET,
    )(*operands)


def whiten(spectra, owners, source_slots):
    return call(
        whiten_kernel,
        (
            jax.ShapeDtypeStruct((N_RECV, PAIRS * RECV_DEV, 128), bf16),
            jax.ShapeDtypeStruct((80, 256), bf16),
        ),
        [spectra, owners, source_slots],
        [HBM] * 3,
        [
            pltpu.VMEM((2, WIN, RECV_DEV, F), bf16),
            pltpu.SMEM((4,), jnp.int32),
            pltpu.SMEM((4, 8), jnp.int32),
            pltpu.VMEM((N_RECV * PAIRS * RECV_DEV, 128), f32),
            pltpu.VMEM((80, 256), f32),
            pltpu.SemaphoreType.DMA((6,)),
        ],
        grant=53,
    )


def cross(pick, channels):
    return call(
        cross_kernel,
        jax.ShapeDtypeStruct((8, 64, 256), bf16),
        [pick, channels],
        [VMEM, VMEM],
        [pltpu.VMEM((2, 512, 128), f32)],
    )


def gather(partial):
    return call(
        gather_kernel,
        jax.ShapeDtypeStruct((2 * N_RECV, 2, 128), f32),
        [partial],
        [VMEM],
        [pltpu.VMEM((256, 128), f32), pltpu.VMEM((2, 64, 128), f32)],
    )


def lags(dofs):
    return call(
        lags_kernel,
        jax.ShapeDtypeStruct((2, RECV_DEV, F), f32),
        [dofs, *transform_table()],
        [VMEM] * 3,
        [pltpu.VMEM((2, 64, 128), f32), pltpu.VMEM((128, 128), f32), pltpu.VMEM((4, 16, 128), f32)],
    )


def per_device(spectra, owners, source_slots):
    exchange = functools.partial(lax.all_to_all, split_axis=0, concat_axis=0, tiled=True)
    mine, pick = whiten(spectra, owners, source_slots)
    channels = exchange(mine, RECV)
    partial = exchange(cross(pick, channels), ("x", "core"))
    return lags(exchange(gather(partial), (*RECV, "y_hi")))


def solution(mesh):
    names = (*RECV, *TM)
    fine = Mesh(mesh.devices.reshape([SIZES[n] for n in names]), names)
    in_specs = (P(None, TM, RECV, None), P(), P())
    out_specs = P(TM, RECV, None)
    return jax.shard_map(
        per_device, mesh=fine, in_specs=in_specs, out_specs=out_specs, check_vma=False
    )
```

time: 531 us -> 67.9 us (0.13)
  waiting for transfers between devices: 407 us -> 0 us
  matrix products: 62.7 us -> 0 us
  blocking collectives: 0 us -> 60.9 us
  local copies, waits for them, and re-layouts: 42.1 us -> 1.35 us
  between operations: 16.1 us -> 0.04 us
    psum x1 -> x0, waiting for transfers between devices: 306 us -> none  [broadcast(): return lax.psum(kept, axis)]
    reduce_scatter x1 -> x0, waiting for transfers between devices: 101 us -> none  [per_device(): lax.psum_scatter(inverse_lags(cross_real, cross_imag, cosine, sine), 'tm'...]
    dot_general x23 -> x0, matrix products: 62.7 us -> none  [the longest x4 14.8 us: per_device(): jnp.einsum('wsf,wrf->srf', arrived[1], whitened[1], preferred_element_typ...]
    all_to_all x0 -> x3, blocking collectives: none -> 60.9 us  [the longest x1 29 us: per_device(): channels = exchange(mine, RECV)]
    squeeze x13 -> x0, local copies, waits for them, and re-layouts: 20.4 us -> none  [the longest x6 11.4 us: per_device(): arrived[1]]
    add x4 -> x0, local copies, waits for them, and re-layouts: 10.7 us -> none  [per_device(): jnp.einsum('wsf,wrf->srf', arrived[0], whitened[0], preferred_element_typ...]
    sub x4 -> x0, local copies, waits for them, and re-layouts: 9.53 us -> none  [per_device(): jnp.einsum('wsf,wrf->srf', arrived[0], whitened[1], preferred_element_typ...]
  transfers between devices with their start and end apart: 2 -> 0, of which waited for: 2 -> 0; matrix products, arithmetic and copies ran while one was open for 0% -> 0% of each run, Pallas kernels for 0% -> 0%
where the time goes in v2:
time: 67.9 us; the launch traced here: 67.6 us
  blocking collectives  60.9 us (90%)
  Pallas kernels  5.31 us (8%)
  local copies, waits for them, and re-layouts  1.35 us (2%)
    all_to_all x1, blocking collectives, per_device(): channels = exchange(mine, RECV)  29 us
    all_to_all x1, blocking collectives, per_device(): return lags(exchange(gather(partial), (*RECV, 'y_hi')))  17.9 us
    all_to_all x1, blocking collectives, per_device(): partial = exchange(cross(pick, channels), ('x', 'core'))  14 us
    pallas_call x4, Pallas kernels, call(): pl.pallas_call(kernel, out_shape=outs, in_specs=specs, out_specs=jax.tree...  5.31 us

profile of v2, /device:TPU:1, one launch (start us, length us, event | category | flops | bytes accessed | tf_op | source)
XLA Modules:
  0.0 67.6 jit_solution(12172559747309454632)
XLA Ops:
  0.0 0.0 copy-start.2
  0.0 0.7 %copy-done.2 = s32[4,8]{1,0:T(4,128)S(1)} copy-done((s32[4,8]{1,0:T(4,128)S(1)}, s32[4,8]{1,0:T(4,128)}, u32[]{:S(2)}) %copy-start.2) | copy-done | bytes 152
  0.7 0.0 copy-start.3
  0.7 0.7 copy-done.3
  1.3 2.6 %shard_map.55 = (bf16[32,64,128]{2,1,0:T(8,128)(2,1)S(1)}, bf16[80,256]{1,0:T(8,128)(2,1)S(1)}) custom-call(bf16[2,32,8,512]{3,2,1,0:T(8,128)(2,1)} %x_hbm.1, s32[4]{0:T(128)S(1)} %copy-done.3, s32[4,8]{1,0:T(4,128)S(1)} %copy-done.2), custom_call_target="tpu_custom_call" | custom-call | tf_op jit(solution)/shard_map/pallas_call | solution.py:250
  4.0 29.0 %all_to_all.15.y_ref = bf16[32,64,128]{2,1,0:T(8,128)(2,1)S(1)} all-to-all(bf16[32,64,128]{2,1,0:T(8,128)(2,1)S(1)} %get-tuple-element.8), channel_id=1, replica_groups=mesh['z'=8,'y_lo'=4,'x'=4,'y_hi'=2,'core'=2] {'z','y_lo'}, dimensions={0} | all-to-all | bytes 1048576 | tf_op jit(solution)/shard_map/all_to_all | solution.py:315
  33.0 0.0 copy-start.1
  33.0 1.3 %shard_map.56 = bf16[8,64,256]{2,1,0:T(8,128)(2,1)S(1)} custom-call(bf16[80,256]{1,0:T(8,128)(2,1)S(1)} %get-tuple-element.7.pick_ref, bf16[32,64,128]{2,1,0:T(8,128)(2,1)S(1)} %all_to_all.15.y_ref), custom_call_target="tpu_custom_call" | custom-call | tf_op jit(solution)/shard_map/pallas_call | solution.py:250
  34.3 0.0 copy-start
  34.3 14.0 %all_to_all.16.z_ref = bf16[8,64,256]{2,1,0:T(8,128)(2,1)S(1)} all-to-all(bf16[8,64,256]{2,1,0:T(8,128)(2,1)S(1)} %shard_map.56), channel_id=1, replica_groups=mesh['z'=8,'y_lo'=4,'x'=4,'y_hi'=2,'core'=2] {'x','core'}, dimensions={0} | all-to-all | bytes 524288 | tf_op jit(solution)/shard_map/all_to_all | solution.py:316
  48.3 0.3 shard_map.57
  48.6 17.9 %all_to_all.17.q_ref = f32[64,2,128]{2,1,0:T(2,128)S(1)} all-to-all(f32[64,2,128]{2,1,0:T(2,128)S(1)} %shard_map.57), channel_id=1, replica_groups=mesh['z'=8,'y_lo'=4,'x'=4,'y_hi'=2,'core'=2] {'z','y_lo','y_hi'}, dimensions={0} | all-to-all | bytes 131072 | tf_op jit(solution)/shard_map/all_to_all | solution.py:317
  66.5 0.0 copy-done.1
  66.5 0.0 copy-done
  66.5 1.1 %shard_map.58 = f32[2,8,512]{2,1,0:T(8,128)} custom-call(f32[64,2,128]{2,1,0:T(2,128)S(1)} %all_to_all.17.q_ref, bf16[64,8,512]{2,1,0:T(8,128)(2,1)S(1)} %copy-done.1, bf16[64,8,512]{2,1,0:T(8,128)(2,1)S(1)} %copy-done), custom_call_target="tpu_custom_call" | custom-call | tf_op jit(solution)/shard_map/pallas_call | solution.py:250
Async XLA Ops:
  0.0 0.7 %copy-start.2 = (s32[4,8]{1,0:T(4,128)S(1)}, s32[4,8]{1,0:T(4,128)}, u32[]{:S(2)}) copy-start(s32[4,8]{1,0:T(4,128)} %slots_hbm.1) | copy-start | bytes 388
  0.7 0.7 copy-start.3
  33.0 33.5 %copy-start.1 = (bf16[64,8,512]{2,1,0:T(8,128)(2,1)S(1)}, bf16[64,8,512]{2,1,0:T(8,128)(2,1)}, u32[]{:S(2)}) copy-start(bf16[64,8,512]{2,1,0:T(8,128)(2,1)} %constant.4.clone.high_ref) | copy-start | bytes 1572868
  34.3 32.2 %copy-start = (bf16[64,8,512]{2,1,0:T(8,128)(2,1)S(1)}, bf16[64,8,512]{2,1,0:T(8,128)(2,1)}, u32[]{:S(2)}) copy-start(bf16[64,8,512]{2,1,0:T(8,128)(2,1)} %constant.5.clone.low_ref) | copy-start | bytes 1572868

commit v3 on v2

--- a/solution.py
+++ b/solution.py
@@ -18,6 +18,7 @@
 WIN = 32
 PAIRS = 8
 EPSILON = 1e-05
+CHUNKS = 2
 INTERPRET = False
 
 RECV = ("z", "y_lo")
@@ -102,54 +103,62 @@
 
 
 def whiten_kernel(
-    x_hbm, owners_hbm, slots_hbm, y_ref, pick_ref, x_ref, owners_ref, slots_ref, tall, pick, sems
+    x_hbm, owners_hbm, slots_hbm, y_ref, pick_ref, x_ref, owners_ref, slots_ref, white, tall, pick, sems
 ):
     is_first = lax.axis_index(RECV) == 0
+    part = WIN // CHUNKS
     copies = [
-        pltpu.make_async_copy(owners_hbm, owners_ref, sems.at[4]),
-        pltpu.make_async_copy(slots_hbm, slots_ref, sems.at[5]),
+        pltpu.make_async_copy(
+            x_hbm.at[:, pl.ds(k * part, part)], x_ref.at[:, pl.ds(k * part, part)], sems.at[k]
+        )
+        for k in range(CHUNKS)
     ]
-    for c in range(2):
-        for part in range(2):
-            here = pl.ds(part * WIN // 2, WIN // 2)
-            copies.append(
-                pltpu.make_async_copy(x_hbm.at[c, here], x_ref.at[c, here], sems.at[2 * c + part])
-            )
-    for copy in copies:
+    small = [
+        pltpu.make_async_copy(owners_hbm, owners_ref, sems.at[CHUNKS]),
+        pltpu.make_async_copy(slots_hbm, slots_ref, sems.at[CHUNKS + 1]),
+    ]
+    for copy in copies + small:
         copy.start()
 
     near = band()
     bins = iota((8, F), 1)
     counts = (jnp.minimum(bins + HALF, F - 1) - jnp.maximum(bins - HALF, 0) + 1).astype(f32)
+    share = (1.0 / counts)[:1]
     row = iota((256, 256), 0)
     column = iota((256, 256), 1)
     forward = ones_where(row == column)
     backward = ones_where((row + column) % 256 == 0)
-    source_row = iota((F, 128), 0)
-    goes_to = (source_row % 8) * 64 + source_row // 8
-    lane = iota((F, 128), 1)
-    lanes = jnp.concatenate([ones_where(goes_to == lane + 128 * b) for b in range(4)], axis=1)
-
-    for copy in copies:
+    low = iota((256, 128), 1) < 64
+
+    rows = part * RECV_DEV
+    for k in range(CHUNKS):
+        copies[k].wait()
+        re, im = [
+            x_ref[c, part * k : part * (k + 1)].astype(f32).reshape(rows, F) for c in range(2)
+        ]
+        energy = re * re + im * im
+        first = energy.astype(bf16)
+        second = (energy - first.astype(f32)).astype(bf16)
+        total = dot(first, near) + dot(second, near)
+        scale = lax.rsqrt(total * share + EPSILON)
+        for c, value in enumerate((re, im)):
+            start = (c * WIN + k * part) * RECV_DEV
+            for b in range(4):
+                white.at[b][start : start + rows, :] = (value * scale)[:, 128 * b : 128 * (b + 1)]
+
+    for copy in small:
         copy.wait()
     source_picker(owners_ref, slots_ref, pick)
     pick[64:80, :] = jnp.full((16, 256), jnp.where(is_first, 1.0, 0.0), f32)
     pick_ref[...] = pick[...].astype(bf16)
 
-    rows = WIN * RECV_DEV
-    re = x_ref[0].astype(f32).reshape(rows, F)
-    im = x_ref[1].astype(f32).reshape(rows, F)
-    energy = re * re + im * im
-    first = energy.astype(bf16)
-    rest = energy - first.astype(f32)
-    second = rest.astype(bf16)
-    third = (rest - second.astype(f32)).astype(bf16)
-    total = dot(first, near) + (dot(second, near) + dot(third, near))
-    scale = lax.rsqrt(total * (1.0 / counts)[:1] + EPSILON)
-    white = jnp.concatenate([(re * scale).astype(bf16), (im * scale).astype(bf16)], axis=0)
-    ahead = dot(dot_nt(forward, white[:, :256]).astype(bf16), lanes)
-    behind = dot(dot_nt(backward, white[:, 256:]).astype(bf16), lanes)
-    low = iota((256, 128), 1) < 64
+    def by_channel(b):
+        strips = [white.at[b][pl.ds(r, 2 * WIN, stride=RECV_DEV), :] for r in range(RECV_DEV)]
+        return jnp.concatenate(strips, axis=0).astype(bf16)
+
+    blocks = [by_channel(b) for b in range(4)]
+    ahead = dot_nt(forward, jnp.concatenate(blocks[:2], axis=1))
+    behind = dot_nt(backward, jnp.concatenate(blocks[2:], axis=1))
     for g in range(4):
         one = ahead[:, 128 * g : 128 * (g + 1)]
         two = behind[:, 128 * g : 128 * (g + 1)]
@@ -242,18 +251,17 @@
 
 
 VMEM = pl.BlockSpec(memory_space=pltpu.VMEM)
-SMEM = pl.BlockSpec(memory_space=pltpu.SMEM)
-HBM = pl.BlockSpec(memory_space=pl.ANY)
-
-
-def call(kernel, outs, operands, specs, scratch=(), grant=32):
+HBM = pl.BlockSpec(memory_space=pltpu.HBM)
+
+
+def call(kernel, outs, operands, specs, scratch=()):
     return pl.pallas_call(
         kernel,
         out_shape=outs,
         in_specs=specs,
         out_specs=jax.tree.map(lambda _: VMEM, outs),
         scratch_shapes=list(scratch),
-        compiler_params=pltpu.CompilerParams(vmem_limit_bytes=grant << 20),
+        compiler_params=pltpu.CompilerParams(vmem_limit_bytes=32 << 20),
         interpret=INTERPRET,
     )(*operands)
 
@@ -265,17 +273,17 @@
             jax.ShapeDtypeStruct((N_RECV, PAIRS * RECV_DEV, 128), bf16),
             jax.ShapeDtypeStruct((80, 256), bf16),
         ),
-        [spectra, owners, source_slots],
+        [pltpu.with_memory_space_constraint(a, pltpu.HBM) for a in (spectra, owners, source_slots)],
         [HBM] * 3,
         [
             pltpu.VMEM((2, WIN, RECV_DEV, F), bf16),
             pltpu.SMEM((4,), jnp.int32),
             pltpu.SMEM((4, 8), jnp.int32),
+            pltpu.VMEM((4, 2 * WIN * RECV_DEV, 128), f32),
             pltpu.VMEM((N_RECV * PAIRS * RECV_DEV, 128), f32),
             pltpu.VMEM((80, 256), f32),
-            pltpu.SemaphoreType.DMA((6,)),
+            pltpu.SemaphoreType.DMA((CHUNKS + 2,)),
         ],
-        grant=53,
     )
 
 

time: 67.9 us -> 66.1 us (0.973)
  local copies, waits for them, and re-layouts: 1.35 us -> 0.01 us
    unnamed x8 -> x4, local copies, waits for them, and re-layouts: 1.35 us -> 0.01 us
where the time goes in v3:
time: 66.1 us; the launch traced here: 65.9 us
  blocking collectives  60.9 us (92%)
  Pallas kernels  4.89 us (7%)
    all_to_all x1, blocking collectives, per_device(): channels = exchange(mine, RECV)  29 us
    all_to_all x1, blocking collectives, per_device(): return lags(exchange(gather(partial), (*RECV, 'y_hi')))  17.9 us
    all_to_all x1, blocking collectives, per_device(): partial = exchange(cross(pick, channels), ('x', 'core'))  14 us
    pallas_call x4, Pallas kernels, call(): pl.pallas_call(kernel, out_shape=outs, in_specs=specs, out_specs=jax.tree...  4.89 us

profile of v3, /device:TPU:1, one launch (start us, length us, event | category | flops | bytes accessed | tf_op | source)
XLA Modules:
  0.0 65.9 jit_solution(17091233585602931958)
XLA Ops:
  0.0 2.2 %shard_map.55 = (bf16[32,64,128]{2,1,0:T(8,128)(2,1)S(1)}, bf16[80,256]{1,0:T(8,128)(2,1)S(1)}) custom-call(bf16[2,32,8,512]{3,2,1,0:T(8,128)(2,1)} %x_hbm.1, s32[4]{0:T(128)} %owners_hbm.1, s32[4,8]{1,0:T(4,128)} %slots_hbm.1), custom_call_target="tpu_custom_call" | custom-call | tf_op jit(solution)/shard_map/pallas_call | solution.py:258
  2.2 29.0 %all_to_all.15.y_ref = bf16[32,64,128]{2,1,0:T(8,128)(2,1)S(1)} all-to-all(bf16[32,64,128]{2,1,0:T(8,128)(2,1)S(1)} %get-tuple-element.8), channel_id=1, replica_groups=mesh['z'=8,'y_lo'=4,'x'=4,'y_hi'=2,'core'=2] {'z','y_lo'}, dimensions={0} | all-to-all | bytes 1048576 | tf_op jit(solution)/shard_map/all_to_all | solution.py:323
  31.2 0.0 copy-start.1
  31.2 1.3 %shard_map.56 = bf16[8,64,256]{2,1,0:T(8,128)(2,1)S(1)} custom-call(bf16[80,256]{1,0:T(8,128)(2,1)S(1)} %get-tuple-element.7.pick_ref, bf16[32,64,128]{2,1,0:T(8,128)(2,1)S(1)} %all_to_all.15.y_ref), custom_call_target="tpu_custom_call" | custom-call | tf_op jit(solution)/shard_map/pallas_call | solution.py:258
  32.5 0.0 copy-start
  32.6 14.0 %all_to_all.16.z_ref = bf16[8,64,256]{2,1,0:T(8,128)(2,1)S(1)} all-to-all(bf16[8,64,256]{2,1,0:T(8,128)(2,1)S(1)} %shard_map.56), channel_id=1, replica_groups=mesh['z'=8,'y_lo'=4,'x'=4,'y_hi'=2,'core'=2] {'x','core'}, dimensions={0} | all-to-all | bytes 524288 | tf_op jit(solution)/shard_map/all_to_all | solution.py:324
  46.5 0.3 shard_map.57
  46.8 17.9 %all_to_all.17.q_ref = f32[64,2,128]{2,1,0:T(2,128)S(1)} all-to-all(f32[64,2,128]{2,1,0:T(2,128)S(1)} %shard_map.57), channel_id=1, replica_groups=mesh['z'=8,'y_lo'=4,'x'=4,'y_hi'=2,'core'=2] {'z','y_lo','y_hi'}, dimensions={0} | all-to-all | bytes 131072 | tf_op jit(solution)/shard_map/all_to_all | solution.py:325
  64.8 0.0 copy-done.1
  64.8 0.0 copy-done
  64.8 1.1 %shard_map.58 = f32[2,8,512]{2,1,0:T(8,128)} custom-call(f32[64,2,128]{2,1,0:T(2,128)S(1)} %all_to_all.17.q_ref, bf16[64,8,512]{2,1,0:T(8,128)(2,1)S(1)} %copy-done.1, bf16[64,8,512]{2,1,0:T(8,128)(2,1)S(1)} %copy-done), custom_call_target="tpu_custom_call" | custom-call | tf_op jit(solution)/shard_map/pallas_call | solution.py:258
Async XLA Ops:
  31.2 33.5 %copy-start.1 = (bf16[64,8,512]{2,1,0:T(8,128)(2,1)S(1)}, bf16[64,8,512]{2,1,0:T(8,128)(2,1)}, u32[]{:S(2)}) copy-start(bf16[64,8,512]{2,1,0:T(8,128)(2,1)} %constant.4.clone.high_ref) | copy-start | bytes 1572868
  32.5 32.2 %copy-start = (bf16[64,8,512]{2,1,0:T(8,128)(2,1)S(1)}, bf16[64,8,512]{2,1,0:T(8,128)(2,1)}, u32[]{:S(2)}) copy-start(bf16[64,8,512]{2,1,0:T(8,128)(2,1)} %constant.5.clone.low_ref) | copy-start | bytes 1572868

commit v4 on v3

--- a/solution.py
+++ b/solution.py
@@ -19,6 +19,7 @@
 PAIRS = 8
 EPSILON = 1e-05
 CHUNKS = 2
+PITCH = 40
 INTERPRET = False
 
 RECV = ("z", "y_lo")
@@ -170,33 +171,52 @@
 def cross_kernel(pick_ref, y_ref, z_ref, wide):
     pick = pick_ref[:64, :]
     is_first = pick_ref[64:80, :128].astype(f32)[:1] > 0.5
-    row = iota((64, 128), 0)
-    lane = iota((64, 128), 1)
-    imaginary = (row // N_TM) % 2 == 1
+    lane = iota((N_TM, 128), 1)
     real_lane = (lane // 32) % 2 == 0
     ahead = lane < 64
     sign = jnp.where(real_lane == ahead, -1.0, 1.0)
-    for p in range(PAIRS):
-        if p % 2 == 0:
-            two = y_ref[:, 8 * p : 8 * p + 16, :].astype(f32)
-        side = two[:, 8 * (p % 2) : 8 * (p % 2) + 8, :].reshape(256, 128).astype(bf16)
-        source = dot(pick, side)
-        turned = sign * jnp.where(real_lane, pltpu.roll(source, 96, 1), pltpu.roll(source, 32, 1))
-        left = jnp.where(imaginary, turned, source)
-        if p == 0:
-            ends = jnp.where(imaginary == ahead, 0.0, source)
-            left = jnp.where(is_first, ends, left)
+    nothing = jnp.zeros((64, 128), f32)
+    for pair in range(PAIRS // 2):
+        two = y_ref[:, 16 * pair : 16 * pair + 16, :].astype(f32)
+        side = jnp.concatenate(
+            [two[:, 8 * i : 8 * i + 8, :].reshape(256, 128) for i in range(2)], axis=1
+        ).astype(bf16)
+        found = dot(pick, side)
+        lefts = []
+        for i in range(2):
+            strips = []
+            for q in range(4):
+                strip = found[N_TM * q : N_TM * (q + 1), 128 * i : 128 * (i + 1)]
+                first_bin = jnp.where(ahead == (q % 2 == 0), strip, 0.0)
+                if q % 2:
+                    strip = sign * jnp.where(
+                        real_lane, pltpu.roll(strip, 96, 1), pltpu.roll(strip, 32, 1)
+                    )
+                if pair == 0 and i == 0:
+                    strip = jnp.where(is_first, first_bin, strip)
+                strips.append(strip)
+            lefts.append(jnp.concatenate(strips, axis=0))
+        left = jnp.concatenate(
+            [
+                jnp.concatenate([lefts[0], nothing], axis=1),
+                jnp.concatenate([nothing, lefts[1]], axis=1),
+            ],
+            axis=0,
+        )
         out = dot_nt(left.astype(bf16), side)
-        for q in range(4):
-            for h in range(2):
-                wide.at[h][pl.ds(8 * q + p, N_TM, stride=32), :] = out[
-                    N_TM * q : N_TM * (q + 1), 128 * h : 128 * (h + 1)
-                ]
+        for i in range(2):
+            for q in range(4):
+                row = 64 * i + N_TM * q
+                for h in range(2):
+                    wide.at[h][pl.ds(8 * q + 2 * pair + i, N_TM, stride=PITCH), :] = out[
+                        row : row + N_TM, 128 * h : 128 * (h + 1)
+                    ]
     for h in range(2):
-        z_ref[:, :, 128 * h : 128 * (h + 1)] = wide[h].astype(bf16).reshape(8, 64, 128)
-
-
-def gather_kernel(z_ref, q_ref, tall, flat):
+        block = wide[h].reshape(N_TM, PITCH, 128)[:, :32, :]
+        z_ref[:, :, 128 * h : 128 * (h + 1)] = block.astype(bf16).reshape(8, 64, 128)
+
+
+def gather_kernel(z_ref, q_ref, tall):
     total = jnp.sum(z_ref[...].astype(f32), axis=0)
     for h in range(2):
         block = total[:, 128 * h : 128 * (h + 1)]
@@ -211,19 +231,11 @@
                 if r != y:
                     moved = pltpu.roll(moved, (32 * (r - y)) % 128, 1)
                 packed = jnp.where(group == r, moved, packed)
-            flat.at[h][pl.ds(y, N_RECV, stride=2), :] = packed
-    for h in range(2):
-        q_ref[:, h, :] = flat[h]
-
-
-def lags_kernel(q_ref, high_ref, low_ref, out_ref, flat, turned, mixed):
-    for h in range(2):
-        flat.at[h][...] = q_ref[:, h, :]
-    sums = []
-    for h in range(2):
-        sums.append(
-            flat.at[h][pl.ds(0, N_RECV, stride=2), :] + flat.at[h][pl.ds(1, N_RECV, stride=2), :]
-        )
+            q_ref[N_RECV * y : N_RECV * (y + 1), h, :] = packed
+
+
+def lags_kernel(q_ref, high_ref, low_ref, out_ref, turned, mixed):
+    sums = [q_ref[:N_RECV, h, :] + q_ref[N_RECV:, h, :] for h in range(2)]
     turned[...] = jnp.concatenate(sums + [jnp.zeros((64, 128), f32)], axis=0).T
     group = iota((8, 128), 1) // 32
     rows = [[], []]
@@ -293,7 +305,7 @@
         jax.ShapeDtypeStruct((8, 64, 256), bf16),
         [pick, channels],
         [VMEM, VMEM],
-        [pltpu.VMEM((2, 512, 128), f32)],
+        [pltpu.VMEM((2, N_TM * PITCH, 128), f32)],
     )
 
 
@@ -303,7 +315,7 @@
         jax.ShapeDtypeStruct((2 * N_RECV, 2, 128), f32),
         [partial],
         [VMEM],
-        [pltpu.VMEM((256, 128), f32), pltpu.VMEM((2, 64, 128), f32)],
+        [pltpu.VMEM((256, 128), f32)],
     )
 
 
@@ -313,7 +325,7 @@
         jax.ShapeDtypeStruct((2, RECV_DEV, F), f32),
         [dofs, *transform_table()],
         [VMEM] * 3,
-        [pltpu.VMEM((2, 64, 128), f32), pltpu.VMEM((128, 128), f32), pltpu.VMEM((4, 16, 128), f32)],
+        [pltpu.VMEM((128, 128), f32), pltpu.VMEM((4, 16, 128), f32)],
     )
 
 
@@ -322,7 +334,7 @@
     mine, pick = whiten(spectra, owners, source_slots)
     channels = exchange(mine, RECV)
     partial = exchange(cross(pick, channels), ("x", "core"))
-    return lags(exchange(gather(partial), (*RECV, "y_hi")))
+    return lags(exchange(gather(partial), ("y_hi", *RECV)))
 
 
 def solution(mesh):

time: 66.1 us -> 65.5 us (level)
    pallas_call x4, Pallas kernels: 4.89 us -> 4.23 us  [call(): pl.pallas_call(kernel, out_shape=outs, in_specs=specs, out_specs=jax.tree...]
where the time goes in v4:
time: 65.5 us; the launch traced here: 65.2 us
  blocking collectives  61 us (93%)
  Pallas kernels  4.23 us (6%)
    all_to_all x1, blocking collectives, per_device(): channels = exchange(mine, RECV)  29 us
    all_to_all x1, blocking collectives, per_device(): return lags(exchange(gather(partial), ('y_hi', *RECV)))  18 us
    all_to_all x1, blocking collectives, per_device(): partial = exchange(cross(pick, channels), ('x', 'core'))  14 us
    pallas_call x4, Pallas kernels, call(): pl.pallas_call(kernel, out_shape=outs, in_specs=specs, out_specs=jax.tree...  4.23 us

profile of v4, /device:TPU:1, one launch (start us, length us, event | category | flops | bytes accessed | tf_op | source)
XLA Modules:
  0.0 65.2 jit_solution(16873501300061722924)
XLA Ops:
  0.0 2.2 %shard_map.55 = (bf16[32,64,128]{2,1,0:T(8,128)(2,1)S(1)}, bf16[80,256]{1,0:T(8,128)(2,1)S(1)}) custom-call(bf16[2,32,8,512]{3,2,1,0:T(8,128)(2,1)} %x_hbm.1, s32[4]{0:T(128)} %owners_hbm.1, s32[4,8]{1,0:T(4,128)} %slots_hbm.1), custom_call_target="tpu_custom_call" | custom-call | tf_op jit(solution)/shard_map/pallas_call | solution.py:270
  2.2 29.0 %all_to_all.15.y_ref = bf16[32,64,128]{2,1,0:T(8,128)(2,1)S(1)} all-to-all(bf16[32,64,128]{2,1,0:T(8,128)(2,1)S(1)} %get-tuple-element.8), channel_id=1, replica_groups=mesh['z'=8,'y_lo'=4,'x'=4,'y_hi'=2,'core'=2] {'z','y_lo'}, dimensions={0} | all-to-all | bytes 1048576 | tf_op jit(solution)/shard_map/all_to_all | solution.py:335
  31.2 0.0 copy-start.1
  31.2 0.7 %shard_map.56 = bf16[8,64,256]{2,1,0:T(8,128)(2,1)S(1)} custom-call(bf16[80,256]{1,0:T(8,128)(2,1)S(1)} %get-tuple-element.7.pick_ref, bf16[32,64,128]{2,1,0:T(8,128)(2,1)S(1)} %all_to_all.15.y_ref), custom_call_target="tpu_custom_call" | custom-call | tf_op jit(solution)/shard_map/pallas_call | solution.py:270
  31.9 0.0 copy-start
  31.9 14.0 %all_to_all.16.z_ref = bf16[8,64,256]{2,1,0:T(8,128)(2,1)S(1)} all-to-all(bf16[8,64,256]{2,1,0:T(8,128)(2,1)S(1)} %shard_map.56), channel_id=1, replica_groups=mesh['z'=8,'y_lo'=4,'x'=4,'y_hi'=2,'core'=2] {'x','core'}, dimensions={0} | all-to-all | bytes 524288 | tf_op jit(solution)/shard_map/all_to_all | solution.py:336
  45.9 0.2 shard_map.57
  46.2 18.0 %all_to_all.17.q_ref = f32[64,2,128]{2,1,0:T(2,128)S(1)} all-to-all(f32[64,2,128]{2,1,0:T(2,128)S(1)} %shard_map.57), channel_id=1, replica_groups=mesh['z'=8,'y_lo'=4,'x'=4,'y_hi'=2,'core'=2] {'y_hi','z','y_lo'}, dimensions={0} | all-to-all | bytes 131072 | tf_op jit(solution)/shard_map/all_to_all | solution.py:337
  64.2 0.0 copy-done.1
  64.2 0.0 copy-done
  64.2 1.1 %shard_map.58 = f32[2,8,512]{2,1,0:T(8,128)} custom-call(f32[64,2,128]{2,1,0:T(2,128)S(1)} %all_to_all.17.q_ref, bf16[64,8,512]{2,1,0:T(8,128)(2,1)S(1)} %copy-done.1, bf16[64,8,512]{2,1,0:T(8,128)(2,1)S(1)} %copy-done), custom_call_target="tpu_custom_call" | custom-call | tf_op jit(solution)/shard_map/pallas_call | solution.py:270
Async XLA Ops:
  31.2 32.9 %copy-start.1 = (bf16[64,8,512]{2,1,0:T(8,128)(2,1)S(1)}, bf16[64,8,512]{2,1,0:T(8,128)(2,1)}, u32[]{:S(2)}) copy-start(bf16[64,8,512]{2,1,0:T(8,128)(2,1)} %constant.4.clone.high_ref) | copy-start | bytes 1572868
  31.9 32.2 %copy-start = (bf16[64,8,512]{2,1,0:T(8,128)(2,1)S(1)}, bf16[64,8,512]{2,1,0:T(8,128)(2,1)}, u32[]{:S(2)}) copy-start(bf16[64,8,512]{2,1,0:T(8,128)(2,1)} %constant.5.clone.low_ref) | copy-start | bytes 1572868

commit v5 on v4

--- a/solution.py
+++ b/solution.py
@@ -18,11 +18,11 @@
 WIN = 32
 PAIRS = 8
 EPSILON = 1e-05
-CHUNKS = 2
 PITCH = 40
 INTERPRET = False
 
 RECV = ("z", "y_lo")
+ORDER = ('y_lo', 'z')
 TM = ("x", "y_hi", "core")
 SIZES = {"z": 8, "y_lo": 4, "x": 4, "y_hi": 2, "core": 2}
 
@@ -46,7 +46,7 @@
     wave = (wave / F).reshape(F // 8, 8, F)
     high = wave.astype(ml_dtypes.bfloat16)
     low = (wave - high.astype(np.float64)).astype(ml_dtypes.bfloat16)
-    return jnp.asarray(high), jnp.asarray(low)
+    return jnp.asarray(np.concatenate([high, low], axis=0))
 
 
 def dot(a, b):
@@ -66,7 +66,7 @@
 
 
 def tm_place(t):
-    return (t // 4) * 4 + (t % 2) * 2 + (t // 2) % 2
+    return (t % 2) * 8 + (t // 4) * 2 + (t // 2) % 2
 
 
 def band():
@@ -93,7 +93,9 @@
                 if place // 8 != half:
                     continue
                 s = 2 * t + odd
-                channel = owners_ref[s // 8] * RECV_DEV + slots_ref[s // 8, s % 8]
+                owner = owners_ref[s // 8]
+                device = (owner % 4) * 8 + owner // 4
+                channel = device * RECV_DEV + slots_ref[s // 8, s % 8]
                 key = jnp.where(sub == place % 8, channel, key)
             found = jnp.concatenate(
                 [jnp.where(key == lane, 1.0, 0.0), jnp.where(key == lane + 128, 1.0, 0.0)], axis=1
@@ -104,19 +106,13 @@
 
 
 def whiten_kernel(
-    x_hbm, owners_hbm, slots_hbm, y_ref, pick_ref, x_ref, owners_ref, slots_ref, white, tall, pick, sems
+    x_hbm, owners_hbm, slots_hbm, y_ref, pick_ref, x_ref, owners_ref, slots_ref, white, pick, sems
 ):
-    is_first = lax.axis_index(RECV) == 0
-    part = WIN // CHUNKS
-    copies = [
-        pltpu.make_async_copy(
-            x_hbm.at[:, pl.ds(k * part, part)], x_ref.at[:, pl.ds(k * part, part)], sems.at[k]
-        )
-        for k in range(CHUNKS)
-    ]
+    is_first = lax.axis_index(ORDER) == 0
+    copies = [pltpu.make_async_copy(x_hbm.at[c], x_ref.at[c], sems.at[c]) for c in range(2)]
     small = [
-        pltpu.make_async_copy(owners_hbm, owners_ref, sems.at[CHUNKS]),
-        pltpu.make_async_copy(slots_hbm, slots_ref, sems.at[CHUNKS + 1]),
+        pltpu.make_async_copy(owners_hbm, owners_ref, sems.at[2]),
+        pltpu.make_async_copy(slots_hbm, slots_ref, sems.at[3]),
     ]
     for copy in copies + small:
         copy.start()
@@ -131,21 +127,19 @@
     backward = ones_where((row + column) % 256 == 0)
     low = iota((256, 128), 1) < 64
 
-    rows = part * RECV_DEV
-    for k in range(CHUNKS):
-        copies[k].wait()
-        re, im = [
-            x_ref[c, part * k : part * (k + 1)].astype(f32).reshape(rows, F) for c in range(2)
-        ]
-        energy = re * re + im * im
-        first = energy.astype(bf16)
-        second = (energy - first.astype(f32)).astype(bf16)
-        total = dot(first, near) + dot(second, near)
-        scale = lax.rsqrt(total * share + EPSILON)
-        for c, value in enumerate((re, im)):
-            start = (c * WIN + k * part) * RECV_DEV
-            for b in range(4):
-                white.at[b][start : start + rows, :] = (value * scale)[:, 128 * b : 128 * (b + 1)]
+    for copy in copies:
+        copy.wait()
+    re, im = [x_ref[c].astype(f32).reshape(WIN * RECV_DEV, F) for c in range(2)]
+    energy = re * re + im * im
+    first = energy.astype(bf16)
+    second = (energy - first.astype(f32)).astype(bf16)
+    total = dot(first, near) + dot(second, near)
+    scale = lax.rsqrt(total * share + EPSILON)
+    for c, value in enumerate((re, im)):
+        scaled = value * scale
+        here = slice(c * WIN * RECV_DEV, (c + 1) * WIN * RECV_DEV)
+        for b in range(4):
+            white.at[b][here, :] = scaled[:, 128 * b : 128 * (b + 1)]
 
     for copy in small:
         copy.wait()
@@ -163,12 +157,13 @@
     for g in range(4):
         one = ahead[:, 128 * g : 128 * (g + 1)]
         two = behind[:, 128 * g : 128 * (g + 1)]
-        tall[pl.ds(2 * g, 256, stride=8), :] = jnp.where(low, one, pltpu.roll(two, 64, 1))
-        tall[pl.ds(2 * g + 1, 256, stride=8), :] = jnp.where(low, pltpu.roll(one, 64, 1), two)
-    y_ref[...] = tall[...].astype(bf16).reshape(y_ref.shape)
-
-
-def cross_kernel(pick_ref, y_ref, z_ref, wide):
+        even = jnp.where(low, one, pltpu.roll(two, 64, 1)).reshape(N_RECV, 8, 128)
+        odd = jnp.where(low, pltpu.roll(one, 64, 1), two).reshape(N_RECV, 8, 128)
+        y_ref[:, 16 * g : 16 * (g + 1), :] = jnp.concatenate([even, odd], axis=1).astype(bf16)
+
+
+def cross_kernel(pick_ref, y_ref, z_ref, wide, tall):
+    tall[...] = y_ref[...].astype(f32).reshape(tall.shape)
     pick = pick_ref[:64, :]
     is_first = pick_ref[64:80, :128].astype(f32)[:1] > 0.5
     lane = iota((N_TM, 128), 1)
@@ -177,9 +172,8 @@
     sign = jnp.where(real_lane == ahead, -1.0, 1.0)
     nothing = jnp.zeros((64, 128), f32)
     for pair in range(PAIRS // 2):
-        two = y_ref[:, 16 * pair : 16 * pair + 16, :].astype(f32)
         side = jnp.concatenate(
-            [two[:, 8 * i : 8 * i + 8, :].reshape(256, 128) for i in range(2)], axis=1
+            [tall[pl.ds(2 * pair + i, 256, stride=8), :] for i in range(2)], axis=1
         ).astype(bf16)
         found = dot(pick, side)
         lefts = []
@@ -231,11 +225,14 @@
                 if r != y:
                     moved = pltpu.roll(moved, (32 * (r - y)) % 128, 1)
                 packed = jnp.where(group == r, moved, packed)
-            q_ref[N_RECV * y : N_RECV * (y + 1), h, :] = packed
-
-
-def lags_kernel(q_ref, high_ref, low_ref, out_ref, turned, mixed):
-    sums = [q_ref[:N_RECV, h, :] + q_ref[N_RECV:, h, :] for h in range(2)]
+            for o in range(4):
+                row = 16 * o + 8 * y
+                q_ref[row : row + 8, h, :] = packed[8 * o : 8 * (o + 1)]
+
+
+def lags_kernel(q_ref, wave_ref, out_ref, turned, mixed):
+    both = [q_ref[:, h, :].reshape(4, 2, 8, 128) for h in range(2)]
+    sums = [(b[:, 0] + b[:, 1]).reshape(N_RECV, 128) for b in both]
     turned[...] = jnp.concatenate(sums + [jnp.zeros((64, 128), f32)], axis=0).T
     group = iota((8, 128), 1) // 32
     rows = [[], []]
@@ -251,8 +248,8 @@
     value = jnp.concatenate([jnp.concatenate(r, axis=1) for r in rows], axis=0)
     first = value.astype(bf16)
     second = (value - first.astype(f32)).astype(bf16)
-    high = high_ref[...].reshape(F, F)
-    low = low_ref[...].reshape(F, F)
+    high = wave_ref[: F // 8].reshape(F, F)
+    low = wave_ref[F // 8 :].reshape(F, F)
     both = dot(jnp.concatenate([first, second], axis=0), high)
     lags = both[:16] + (both[16:] + dot(first, low))
     for b in range(4):
@@ -292,9 +289,8 @@
             pltpu.SMEM((4,), jnp.int32),
             pltpu.SMEM((4, 8), jnp.int32),
             pltpu.VMEM((4, 2 * WIN * RECV_DEV, 128), f32),
-            pltpu.VMEM((N_RECV * PAIRS * RECV_DEV, 128), f32),
             pltpu.VMEM((80, 256), f32),
-            pltpu.SemaphoreType.DMA((CHUNKS + 2,)),
+            pltpu.SemaphoreType.DMA((4,)),
         ],
     )
 
@@ -305,7 +301,7 @@
         jax.ShapeDtypeStruct((8, 64, 256), bf16),
         [pick, channels],
         [VMEM, VMEM],
-        [pltpu.VMEM((2, N_TM * PITCH, 128), f32)],
+        [pltpu.VMEM((2, N_TM * PITCH, 128), f32), pltpu.VMEM((2048, 128), f32)],
     )
 
 
@@ -323,8 +319,8 @@
     return call(
         lags_kernel,
         jax.ShapeDtypeStruct((2, RECV_DEV, F), f32),
-        [dofs, *transform_table()],
-        [VMEM] * 3,
+        [dofs, transform_table()],
+        [VMEM] * 2,
         [pltpu.VMEM((128, 128), f32), pltpu.VMEM((4, 16, 128), f32)],
     )
 
@@ -332,9 +328,9 @@
 def per_device(spectra, owners, source_slots):
     exchange = functools.partial(lax.all_to_all, split_axis=0, concat_axis=0, tiled=True)
     mine, pick = whiten(spectra, owners, source_slots)
-    channels = exchange(mine, RECV)
-    partial = exchange(cross(pick, channels), ("x", "core"))
-    return lags(exchange(gather(partial), ("y_hi", *RECV)))
+    channels = exchange(mine, ORDER)
+    partial = exchange(cross(pick, channels), ('core', 'x'))
+    return lags(exchange(gather(partial), ("y_lo", "y_hi", "z")))
 
 
 def solution(mesh):

time: 65.5 us -> 64.7 us (0.988)
  no operation moved by 1% of the time
where the time goes in v5:
time: 64.7 us; the launch traced here: 64.5 us
  blocking collectives  60.4 us (93%)
  Pallas kernels  4.1 us (6%)
    all_to_all x1, blocking collectives, per_device(): channels = exchange(mine, ORDER)  29 us
    all_to_all x1, blocking collectives, per_device(): return lags(exchange(gather(partial), ('y_lo', 'y_hi', 'z')))  17.8 us
    all_to_all x1, blocking collectives, per_device(): partial = exchange(cross(pick, channels), ('core', 'x'))  13.6 us
    pallas_call x4, Pallas kernels, call(): pl.pallas_call(kernel, out_shape=outs, in_specs=specs, out_specs=jax.tree...  4.1 us

profile of v5, /device:TPU:1, one launch (start us, length us, event | category | flops | bytes accessed | tf_op | source)
XLA Modules:
  0.0 64.5 jit_solution(3459258140400961395)
XLA Ops:
  0.0 2.0 %shard_map.46 = (bf16[32,64,128]{2,1,0:T(8,128)(2,1)S(1)}, bf16[80,256]{1,0:T(8,128)(2,1)S(1)}) custom-call(bf16[2,32,8,512]{3,2,1,0:T(8,128)(2,1)} %x_hbm.1, s32[4]{0:T(128)} %owners_hbm.1, s32[4,8]{1,0:T(4,128)} %slots_hbm.1), custom_call_target="tpu_custom_call" | custom-call | tf_op jit(solution)/shard_map/pallas_call | solution.py:267
  2.0 29.0 %all_to_all.15.y_ref = bf16[32,64,128]{2,1,0:T(8,128)(2,1)S(1)} all-to-all(bf16[32,64,128]{2,1,0:T(8,128)(2,1)S(1)} %get-tuple-element.8), channel_id=1, replica_groups=mesh['z'=8,'y_lo'=4,'x'=4,'y_hi'=2,'core'=2] {'y_lo','z'}, dimensions={0} | all-to-all | bytes 1048576 | tf_op jit(solution)/shard_map/all_to_all | solution.py:331
  31.0 0.0 copy-start
  31.0 0.8 %shard_map.47 = bf16[8,64,256]{2,1,0:T(8,128)(2,1)S(1)} custom-call(bf16[80,256]{1,0:T(8,128)(2,1)S(1)} %get-tuple-element.7.pick_ref, bf16[32,64,128]{2,1,0:T(8,128)(2,1)S(1)} %all_to_all.15.y_ref), custom_call_target="tpu_custom_call" | custom-call | tf_op jit(solution)/shard_map/pallas_call | solution.py:267
  31.8 13.6 %all_to_all.16.z_ref = bf16[8,64,256]{2,1,0:T(8,128)(2,1)S(1)} all-to-all(bf16[8,64,256]{2,1,0:T(8,128)(2,1)S(1)} %shard_map.47), channel_id=1, replica_groups=mesh['z'=8,'y_lo'=4,'x'=4,'y_hi'=2,'core'=2] {'core','x'}, dimensions={0} | all-to-all | bytes 524288 | tf_op jit(solution)/shard_map/all_to_all | solution.py:332
  45.3 0.2 shard_map.48
  45.6 17.8 %all_to_all.17.q_ref = f32[64,2,128]{2,1,0:T(2,128)S(1)} all-to-all(f32[64,2,128]{2,1,0:T(2,128)S(1)} %shard_map.48), channel_id=1, replica_groups=mesh['z'=8,'y_lo'=4,'x'=4,'y_hi'=2,'core'=2] {'y_lo','y_hi','z'}, dimensions={0} | all-to-all | bytes 131072 | tf_op jit(solution)/shard_map/all_to_all | solution.py:333
  63.4 0.0 copy-done
  63.4 1.1 %shard_map.49 = f32[2,8,512]{2,1,0:T(8,128)} custom-call(f32[64,2,128]{2,1,0:T(2,128)S(1)} %all_to_all.17.q_ref, bf16[128,8,512]{2,1,0:T(8,128)(2,1)S(1)} %copy-done), custom_call_target="tpu_custom_call" | custom-call | tf_op jit(solution)/shard_map/pallas_call | solution.py:267
Async XLA Ops:
  31.0 32.5 %copy-start = (bf16[128,8,512]{2,1,0:T(8,128)(2,1)S(1)}, bf16[128,8,512]{2,1,0:T(8,128)(2,1)}, u32[]{:S(2)}) copy-start(bf16[128,8,512]{2,1,0:T(8,128)(2,1)} %constant.2.clone.wave_ref) | copy-start | bytes 3145732

commit v6 on v5

--- a/solution.py
+++ b/solution.py
@@ -163,7 +163,8 @@
 
 
 def cross_kernel(pick_ref, y_ref, z_ref, wide, tall):
-    tall[...] = y_ref[...].astype(f32).reshape(tall.shape)
+    rows = N_RECV * PAIRS * RECV_DEV
+    tall[:rows, :] = y_ref[...].astype(f32).reshape(rows, 128)
     pick = pick_ref[:64, :]
     is_first = pick_ref[64:80, :128].astype(f32)[:1] > 0.5
     lane = iota((N_TM, 128), 1)
@@ -206,7 +207,7 @@
                         row : row + N_TM, 128 * h : 128 * (h + 1)
                     ]
     for h in range(2):
-        block = wide[h].reshape(N_TM, PITCH, 128)[:, :32, :]
+        block = wide[h, : N_TM * PITCH, :].reshape(N_TM, PITCH, 128)[:, :32, :]
         z_ref[:, :, 128 * h : 128 * (h + 1)] = block.astype(bf16).reshape(8, 64, 128)
 
 
@@ -233,7 +234,7 @@
 def lags_kernel(q_ref, wave_ref, out_ref, turned, mixed):
     both = [q_ref[:, h, :].reshape(4, 2, 8, 128) for h in range(2)]
     sums = [(b[:, 0] + b[:, 1]).reshape(N_RECV, 128) for b in both]
-    turned[...] = jnp.concatenate(sums + [jnp.zeros((64, 128), f32)], axis=0).T
+    turned[:128, :] = jnp.concatenate(sums + [jnp.zeros((64, 128), f32)], axis=0).T
     group = iota((8, 128), 1) // 32
     rows = [[], []]
     for q in range(4):
@@ -253,7 +254,7 @@
     both = dot(jnp.concatenate([first, second], axis=0), high)
     lags = both[:16] + (both[16:] + dot(first, low))
     for b in range(4):
-        mixed.at[b][...] = lags[:, 128 * b : 128 * (b + 1)]
+        mixed.at[b][:16, :] = lags[:, 128 * b : 128 * (b + 1)]
     for s in range(2):
         for b in range(4):
             out_ref[s, :, 128 * b : 128 * (b + 1)] = mixed.at[b][pl.ds(s, 8, stride=2), :]
@@ -288,7 +289,7 @@
             pltpu.VMEM((2, WIN, RECV_DEV, F), bf16),
             pltpu.SMEM((4,), jnp.int32),
             pltpu.SMEM((4, 8), jnp.int32),
-            pltpu.VMEM((4, 2 * WIN * RECV_DEV, 128), f32),
+            pltpu.VMEM((4, 2 * WIN * RECV_DEV + 8, 128), f32),
             pltpu.VMEM((80, 256), f32),
             pltpu.SemaphoreType.DMA((4,)),
         ],
@@ -301,7 +302,10 @@
         jax.ShapeDtypeStruct((8, 64, 256), bf16),
         [pick, channels],
         [VMEM, VMEM],
-        [pltpu.VMEM((2, N_TM * PITCH, 128), f32), pltpu.VMEM((2048, 128), f32)],
+        [
+            pltpu.VMEM((2, (N_TM + 1) * PITCH, 128), f32),
+            pltpu.VMEM((N_RECV * PAIRS * RECV_DEV + 8, 128), f32),
+        ],
     )
 
 
@@ -311,7 +315,7 @@
         jax.ShapeDtypeStruct((2 * N_RECV, 2, 128), f32),
         [partial],
         [VMEM],
-        [pltpu.VMEM((256, 128), f32)],
+        [pltpu.VMEM((256 + 8, 128), f32)],
     )
 
 
@@ -321,7 +325,7 @@
         jax.ShapeDtypeStruct((2, RECV_DEV, F), f32),
         [dofs, transform_table()],
         [VMEM] * 2,
-        [pltpu.VMEM((128, 128), f32), pltpu.VMEM((4, 16, 128), f32)],
+        [pltpu.VMEM((128 + 16, 128), f32), pltpu.VMEM((4, 16 + 8, 128), f32)],
     )
 
 

time: 64.7 us -> 64.7 us (level)
  no operation moved by 1% of the time
where the time goes in v6:
time: 64.7 us; the launch traced here: 64.5 us
  blocking collectives  60.4 us (93%)
  Pallas kernels  4.1 us (6%)
    all_to_all x1, blocking collectives, per_device(): channels = exchange(mine, ORDER)  29 us
    all_to_all x1, blocking collectives, per_device(): return lags(exchange(gather(partial), ('y_lo', 'y_hi', 'z')))  17.8 us
    all_to_all x1, blocking collectives, per_device(): partial = exchange(cross(pick, channels), ('core', 'x'))  13.5 us
    pallas_call x4, Pallas kernels, call(): pl.pallas_call(kernel, out_shape=outs, in_specs=specs, out_specs=jax.tree...  4.1 us

profile of v6, /device:TPU:1, one launch (start us, length us, event | category | flops | bytes accessed | tf_op | source)
XLA Modules:
  0.0 64.5 jit_solution(12554262848722663924)
XLA Ops:
  0.0 2.0 %shard_map.46 = (bf16[32,64,128]{2,1,0:T(8,128)(2,1)S(1)}, bf16[80,256]{1,0:T(8,128)(2,1)S(1)}) custom-call(bf16[2,32,8,512]{3,2,1,0:T(8,128)(2,1)} %x_hbm.1, s32[4]{0:T(128)} %owners_hbm.1, s32[4,8]{1,0:T(4,128)} %slots_hbm.1), custom_call_target="tpu_custom_call" | custom-call | tf_op jit(solution)/shard_map/pallas_call | solution.py:268
  2.0 29.0 %all_to_all.15.y_ref = bf16[32,64,128]{2,1,0:T(8,128)(2,1)S(1)} all-to-all(bf16[32,64,128]{2,1,0:T(8,128)(2,1)S(1)} %get-tuple-element.8), channel_id=1, replica_groups=mesh['z'=8,'y_lo'=4,'x'=4,'y_hi'=2,'core'=2] {'y_lo','z'}, dimensions={0} | all-to-all | bytes 1048576 | tf_op jit(solution)/shard_map/all_to_all | solution.py:335
  31.0 0.0 copy-start
  31.0 0.8 %shard_map.47 = bf16[8,64,256]{2,1,0:T(8,128)(2,1)S(1)} custom-call(bf16[80,256]{1,0:T(8,128)(2,1)S(1)} %get-tuple-element.7.pick_ref, bf16[32,64,128]{2,1,0:T(8,128)(2,1)S(1)} %all_to_all.15.y_ref), custom_call_target="tpu_custom_call" | custom-call | tf_op jit(solution)/shard_map/pallas_call | solution.py:268
  31.8 13.5 %all_to_all.16.z_ref = bf16[8,64,256]{2,1,0:T(8,128)(2,1)S(1)} all-to-all(bf16[8,64,256]{2,1,0:T(8,128)(2,1)S(1)} %shard_map.47), channel_id=1, replica_groups=mesh['z'=8,'y_lo'=4,'x'=4,'y_hi'=2,'core'=2] {'core','x'}, dimensions={0} | all-to-all | bytes 524288 | tf_op jit(solution)/shard_map/all_to_all | solution.py:336
  45.3 0.2 shard_map.48
  45.6 17.8 %all_to_all.17.q_ref = f32[64,2,128]{2,1,0:T(2,128)S(1)} all-to-all(f32[64,2,128]{2,1,0:T(2,128)S(1)} %shard_map.48), channel_id=1, replica_groups=mesh['z'=8,'y_lo'=4,'x'=4,'y_hi'=2,'core'=2] {'y_lo','y_hi','z'}, dimensions={0} | all-to-all | bytes 131072 | tf_op jit(solution)/shard_map/all_to_all | solution.py:337
  63.4 0.0 copy-done
  63.4 1.1 %shard_map.49 = f32[2,8,512]{2,1,0:T(8,128)} custom-call(f32[64,2,128]{2,1,0:T(2,128)S(1)} %all_to_all.17.q_ref, bf16[128,8,512]{2,1,0:T(8,128)(2,1)S(1)} %copy-done), custom_call_target="tpu_custom_call" | custom-call | tf_op jit(solution)/shard_map/pallas_call | solution.py:268
Async XLA Ops:
  31.0 32.4 %copy-start = (bf16[128,8,512]{2,1,0:T(8,128)(2,1)S(1)}, bf16[128,8,512]{2,1,0:T(8,128)(2,1)}, u32[]{:S(2)}) copy-start(bf16[128,8,512]{2,1,0:T(8,128)(2,1)} %constant.2.clone.wave_ref) | copy-start | bytes 3145732

commit v7 on v6

--- a/solution.py
+++ b/solution.py
@@ -127,10 +127,12 @@
     backward = ones_where((row + column) % 256 == 0)
     low = iota((256, 128), 1) < 64
 
-    for copy in copies:
-        copy.wait()
-    re, im = [x_ref[c].astype(f32).reshape(WIN * RECV_DEV, F) for c in range(2)]
-    energy = re * re + im * im
+    copies[0].wait()
+    re = x_ref[0].astype(f32).reshape(WIN * RECV_DEV, F)
+    energy = re * re
+    copies[1].wait()
+    im = x_ref[1].astype(f32).reshape(WIN * RECV_DEV, F)
+    energy = energy + im * im
     first = energy.astype(bf16)
     second = (energy - first.astype(f32)).astype(bf16)
     total = dot(first, near) + dot(second, near)
@@ -172,11 +174,15 @@
     ahead = lane < 64
     sign = jnp.where(real_lane == ahead, -1.0, 1.0)
     nothing = jnp.zeros((64, 128), f32)
-    for pair in range(PAIRS // 2):
-        side = jnp.concatenate(
+    sides = [
+        jnp.concatenate(
             [tall[pl.ds(2 * pair + i, 256, stride=8), :] for i in range(2)], axis=1
         ).astype(bf16)
-        found = dot(pick, side)
+        for pair in range(PAIRS // 2)
+    ]
+    every = dot(pick, jnp.concatenate(sides, axis=1))
+    for pair, side in enumerate(sides):
+        found = every[:, 256 * pair : 256 * (pair + 1)]
         lefts = []
         for i in range(2):
             strips = []
@@ -214,8 +220,7 @@
 def gather_kernel(z_ref, q_ref, tall):
     total = jnp.sum(z_ref[...].astype(f32), axis=0)
     for h in range(2):
-        block = total[:, 128 * h : 128 * (h + 1)]
-        tall[128 * h : 128 * (h + 1), :] = jnp.concatenate([block, jnp.zeros_like(block)], axis=0).T
+        tall[128 * h : 128 * (h + 1), :64] = total[:, 128 * h : 128 * (h + 1)].T
     group = iota((N_RECV, 128), 1) // 32
     for h in range(2):
         channels = [tall[pl.ds(4 * h + r, N_RECV, stride=8), :] for r in range(4)]
@@ -234,7 +239,7 @@
 def lags_kernel(q_ref, wave_ref, out_ref, turned, mixed):
     both = [q_ref[:, h, :].reshape(4, 2, 8, 128) for h in range(2)]
     sums = [(b[:, 0] + b[:, 1]).reshape(N_RECV, 128) for b in both]
-    turned[:128, :] = jnp.concatenate(sums + [jnp.zeros((64, 128), f32)], axis=0).T
+    turned[:128, :64] = jnp.concatenate(sums, axis=0).T
     group = iota((8, 128), 1) // 32
     rows = [[], []]
     for q in range(4):

time: 64.7 us -> 64.5 us (level)
  no operation moved by 1% of the time
where the time goes in v7:
time: 64.5 us; the launch traced here: 64.3 us
  blocking collectives  60.4 us (94%)
  Pallas kernels  3.92 us (6%)
    all_to_all x1, blocking collectives, per_device(): channels = exchange(mine, ORDER)  29 us
    all_to_all x1, blocking collectives, per_device(): return lags(exchange(gather(partial), ('y_lo', 'y_hi', 'z')))  17.8 us
    all_to_all x1, blocking collectives, per_device(): partial = exchange(cross(pick, channels), ('core', 'x'))  13.6 us
    pallas_call x4, Pallas kernels, call(): pl.pallas_call(kernel, out_shape=outs, in_specs=specs, out_specs=jax.tree...  3.92 us

profile of v7, /device:TPU:1, one launch (start us, length us, event | category | flops | bytes accessed | tf_op | source)
XLA Modules:
  0.0 64.3 jit_solution(17522252276231864012)
XLA Ops:
  0.0 2.0 %shard_map.46 = (bf16[32,64,128]{2,1,0:T(8,128)(2,1)S(1)}, bf16[80,256]{1,0:T(8,128)(2,1)S(1)}) custom-call(bf16[2,32,8,512]{3,2,1,0:T(8,128)(2,1)} %x_hbm.1, s32[4]{0:T(128)} %owners_hbm.1, s32[4,8]{1,0:T(4,128)} %slots_hbm.1), custom_call_target="tpu_custom_call" | custom-call | tf_op jit(solution)/shard_map/pallas_call | solution.py:273
  2.0 29.0 %all_to_all.15.y_ref = bf16[32,64,128]{2,1,0:T(8,128)(2,1)S(1)} all-to-all(bf16[32,64,128]{2,1,0:T(8,128)(2,1)S(1)} %get-tuple-element.8), channel_id=1, replica_groups=mesh['z'=8,'y_lo'=4,'x'=4,'y_hi'=2,'core'=2] {'y_lo','z'}, dimensions={0} | all-to-all | bytes 1048576 | tf_op jit(solution)/shard_map/all_to_all | solution.py:340
  31.0 0.0 copy-start
  31.0 0.6 shard_map.47
  31.6 13.6 %all_to_all.16.z_ref = bf16[8,64,256]{2,1,0:T(8,128)(2,1)S(1)} all-to-all(bf16[8,64,256]{2,1,0:T(8,128)(2,1)S(1)} %shard_map.47), channel_id=1, replica_groups=mesh['z'=8,'y_lo'=4,'x'=4,'y_hi'=2,'core'=2] {'core','x'}, dimensions={0} | all-to-all | bytes 524288 | tf_op jit(solution)/shard_map/all_to_all | solution.py:341
  45.1 0.2 shard_map.48
  45.4 17.8 %all_to_all.17.q_ref = f32[64,2,128]{2,1,0:T(2,128)S(1)} all-to-all(f32[64,2,128]{2,1,0:T(2,128)S(1)} %shard_map.48), channel_id=1, replica_groups=mesh['z'=8,'y_lo'=4,'x'=4,'y_hi'=2,'core'=2] {'y_lo','y_hi','z'}, dimensions={0} | all-to-all | bytes 131072 | tf_op jit(solution)/shard_map/all_to_all | solution.py:342
  63.2 0.0 copy-done
  63.2 1.1 %shard_map.49 = f32[2,8,512]{2,1,0:T(8,128)} custom-call(f32[64,2,128]{2,1,0:T(2,128)S(1)} %all_to_all.17.q_ref, bf16[128,8,512]{2,1,0:T(8,128)(2,1)S(1)} %copy-done), custom_call_target="tpu_custom_call" | custom-call | tf_op jit(solution)/shard_map/pallas_call | solution.py:273
Async XLA Ops:
  31.0 32.3 %copy-start = (bf16[128,8,512]{2,1,0:T(8,128)(2,1)S(1)}, bf16[128,8,512]{2,1,0:T(8,128)(2,1)}, u32[]{:S(2)}) copy-start(bf16[128,8,512]{2,1,0:T(8,128)(2,1)} %constant.2.clone.wave_ref) | copy-start | bytes 3145732

commit v8 on v7

--- a/solution.py
+++ b/solution.py
@@ -167,7 +167,7 @@
 def cross_kernel(pick_ref, y_ref, z_ref, wide, tall):
     rows = N_RECV * PAIRS * RECV_DEV
     tall[:rows, :] = y_ref[...].astype(f32).reshape(rows, 128)
-    pick = pick_ref[:64, :]
+    pick = jnp.concatenate([pick_ref[:16, :], pick_ref[32:48, :]], axis=0)
     is_first = pick_ref[64:80, :128].astype(f32)[:1] > 0.5
     lane = iota((N_TM, 128), 1)
     real_lane = (lane // 32) % 2 == 0
@@ -187,7 +187,7 @@
         for i in range(2):
             strips = []
             for q in range(4):
-                strip = found[N_TM * q : N_TM * (q + 1), 128 * i : 128 * (i + 1)]
+                strip = found[N_TM * (q // 2) : N_TM * (q // 2 + 1), 128 * i : 128 * (i + 1)]
                 first_bin = jnp.where(ahead == (q % 2 == 0), strip, 0.0)
                 if q % 2:
                     strip = sign * jnp.where(

time: 64.5 us -> 64.5 us (level)
  no operation moved by 1% of the time
where the time goes in v8:
time: 64.5 us; the launch traced here: 64.3 us
  blocking collectives  60.4 us (94%)
  Pallas kernels  3.91 us (6%)
    all_to_all x1, blocking collectives, per_device(): channels = exchange(mine, ORDER)  29 us
    all_to_all x1, blocking collectives, per_device(): return lags(exchange(gather(partial), ('y_lo', 'y_hi', 'z')))  17.8 us
    all_to_all x1, blocking collectives, per_device(): partial = exchange(cross(pick, channels), ('core', 'x'))  13.6 us
    pallas_call x4, Pallas kernels, call(): pl.pallas_call(kernel, out_shape=outs, in_specs=specs, out_specs=jax.tree...  3.91 us

profile of v8, /device:TPU:1, one launch (start us, length us, event | category | flops | bytes accessed | tf_op | source)
XLA Modules:
  0.0 64.3 jit_solution(8271925357620670131)
XLA Ops:
  0.0 2.0 %shard_map.46 = (bf16[32,64,128]{2,1,0:T(8,128)(2,1)S(1)}, bf16[80,256]{1,0:T(8,128)(2,1)S(1)}) custom-call(bf16[2,32,8,512]{3,2,1,0:T(8,128)(2,1)} %x_hbm.1, s32[4]{0:T(128)} %owners_hbm.1, s32[4,8]{1,0:T(4,128)} %slots_hbm.1), custom_call_target="tpu_custom_call" | custom-call | tf_op jit(solution)/shard_map/pallas_call | solution.py:273
  2.0 29.0 %all_to_all.15.y_ref = bf16[32,64,128]{2,1,0:T(8,128)(2,1)S(1)} all-to-all(bf16[32,64,128]{2,1,0:T(8,128)(2,1)S(1)} %get-tuple-element.8), channel_id=1, replica_groups=mesh['z'=8,'y_lo'=4,'x'=4,'y_hi'=2,'core'=2] {'y_lo','z'}, dimensions={0} | all-to-all | bytes 1048576 | tf_op jit(solution)/shard_map/all_to_all | solution.py:340
  31.0 0.0 copy-start
  31.0 0.6 shard_map.47
  31.6 13.6 %all_to_all.16.z_ref = bf16[8,64,256]{2,1,0:T(8,128)(2,1)S(1)} all-to-all(bf16[8,64,256]{2,1,0:T(8,128)(2,1)S(1)} %shard_map.47), channel_id=1, replica_groups=mesh['z'=8,'y_lo'=4,'x'=4,'y_hi'=2,'core'=2] {'core','x'}, dimensions={0} | all-to-all | bytes 524288 | tf_op jit(solution)/shard_map/all_to_all | solution.py:341
  45.1 0.2 shard_map.48
  45.4 17.8 %all_to_all.17.q_ref = f32[64,2,128]{2,1,0:T(2,128)S(1)} all-to-all(f32[64,2,128]{2,1,0:T(2,128)S(1)} %shard_map.48), channel_id=1, replica_groups=mesh['z'=8,'y_lo'=4,'x'=4,'y_hi'=2,'core'=2] {'y_lo','y_hi','z'}, dimensions={0} | all-to-all | bytes 131072 | tf_op jit(solution)/shard_map/all_to_all | solution.py:342
  63.2 0.0 copy-done
  63.2 1.1 %shard_map.49 = f32[2,8,512]{2,1,0:T(8,128)} custom-call(f32[64,2,128]{2,1,0:T(2,128)S(1)} %all_to_all.17.q_ref, bf16[128,8,512]{2,1,0:T(8,128)(2,1)S(1)} %copy-done), custom_call_target="tpu_custom_call" | custom-call | tf_op jit(solution)/shard_map/pallas_call | solution.py:273
Async XLA Ops:
  31.0 32.3 %copy-start = (bf16[128,8,512]{2,1,0:T(8,128)(2,1)S(1)}, bf16[128,8,512]{2,1,0:T(8,128)(2,1)}, u32[]{:S(2)}) copy-start(bf16[128,8,512]{2,1,0:T(8,128)(2,1)} %constant.2.clone.wave_ref) | copy-start | bytes 3145732
